TPU v7x, 256 devices: a whole 4x4x8 slice. The times are simulated.
256 devices in a mesh: pre: 8 (over z), dec: 16 (over y, x), rep: 2 (over core).
Axes of the slice: x: 4, y: 4, z: 8, core: 2. Of those that a mesh axis runs over, the one named last changes fastest.
Arguments:
- queries: bfloat16 [96, 256, 8192], P(('rep', 'pre'), None, 'dec'), parts along dimension 0, may hold values from -0.59765625 to 0.59765625
- keys: bfloat16 [96, 256, 8192], P(('rep', 'pre'), None, 'dec'), parts along dimension 0, may hold values from -1.5 to 1.5
- values: bfloat16 [96, 256, 8192], P(('rep', 'pre'), None, 'dec'), parts along dimension 0, may hold values from -6 to 6
- log_decay: float32 [96, 256, 64], P(('rep', 'pre'), None, 'dec'), parts along dimension 0, may hold values from -2 to 0
- prior_state: float32 [96, 64, 128, 128], P(('rep', 'pre'), 'dec'), parts along dimension 0, may hold values from -6 to 6
- lengths: int32 [96], P(('rep', 'pre')), parts along dimension 0, may hold values from 1 to 256, 6272 in all
- owners: int32 [96, 1], P(('rep', 'pre')), parts along dimension 0, may hold values from 0 to 15; in each aligned block of 6 rows (0 to 5, 6 to 11, ...) no two rows name the same one
Outputs:
- prefill_out: bfloat16 [96, 256, 8192], P(('rep', 'pre'), None, 'dec'), parts along dimension 0
- decode_state: float32 [256, 64, 128, 128], P(('rep', 'dec'), 'pre'), parts along dimension 0
There are 2 independent parts, one for each index of `rep`. A program takes and returns all parts, laid end to end along the dimension named above; each array names one. Nothing has to cross between parts.
Inputs may be any that keep to these rules, and one draw needn't show every extreme that they name: `owners`: in each aligned block of 6 rows no owner stands more than 1 times, and some owner exactly so often; every owner stands somewhere. The lengths sum to 48 * 256 // 2 + 256 // 2; the longest is 256.
All inputs are finite; a program needn't handle non-finite values. No bound on the sum of `lengths` on one device may be relied on, other than what follows from the above.
Results may differ from a plain program's by a relative error of at most 0.0047.
Values sent between devices are 32-bit elements; how exact they have to be, the bound alone decides.
No kernel may reach another device: no remote copies, remote signals or barrier semaphores. Data moves between devices by JAX's collectives and lax.ppermute only.
A program may use at most 128 MiB of HBM per device.

v0:
```python
import jax
import jax.numpy as jnp
from jax import lax
from jax.sharding import PartitionSpec as P


def decay_sums(log_decay, lengths):
    tail_length = log_decay.shape[1]
    steps = lax.broadcasted_iota(jnp.int32, (1, tail_length), 1)
    live = (steps < lengths[:, None]).astype(jnp.float32)
    total = jnp.cumsum(log_decay * live[:, :, None], axis=1)
    return (live, total)


def span_output(queries, keys, values, prior_state, live, total):
    prompt_batch, tail_length, width = queries.shape
    head_count = total.shape[2]
    block_size = width // head_count
    qmat = queries.reshape(prompt_batch, tail_length, head_count, block_size)
    kmat = keys.reshape(prompt_batch, tail_length, head_count, block_size)
    value_matrix = values.reshape(prompt_batch, tail_length, head_count, block_size)
    score = jnp.einsum("rthc,rshc->rhts", qmat, kmat, preferred_element_type=jnp.float32)
    lagged = jnp.swapaxes(total, 1, 2)
    steps = jnp.arange(tail_length, dtype=jnp.int32)
    causal = steps[:, None] >= steps[None, :]
    gap = lagged[:, :, :, None] - lagged[:, :, None, :]
    fading = jnp.exp(jnp.where(causal[None, None], gap, -jnp.inf))
    decay_weight = (score * fading * live[:, None, None, :]).astype(jnp.bfloat16)
    inner_product = jnp.einsum(
        "fijv,fvil->fjil", decay_weight, value_matrix, preferred_element_type=jnp.float32
    )
    carried = jnp.einsum(
        "rthc,rhcd->rthd", qmat.astype(jnp.float32), prior_state, precision=lax.Precision.HIGHEST
    )
    carried = carried * jnp.exp(total)[:, :, :, None]
    output = (inner_product + carried) * live[:, :, None, None]
    return output.astype(jnp.bfloat16).reshape(prompt_batch, tail_length, width)


def span_state(keys, values, prior_state, live, total):
    prompt_batch, tail_length, width = keys.shape
    head_count = total.shape[2]
    block_size = width // head_count
    kmat = keys.reshape(prompt_batch, tail_length, head_count, block_size)
    value_matrix = values.reshape(prompt_batch, tail_length, head_count, block_size)
    last = total[:, -1, :]
    keep = jnp.exp(last[:, None, :] - total) * live[:, :, None]
    decayed_state = (kmat.astype(jnp.float32) * keep[:, :, :, None]).astype(jnp.bfloat16)
    fresh_state = jnp.einsum(
        "lmkw,lmkf->lkwf", decayed_state, value_matrix, preferred_element_type=jnp.float32
    )
    return jnp.exp(last)[:, :, None, None] * prior_state + fresh_state


def owner_rank(owners):
    owned = owners[:, 0]
    count = owned.shape[0]
    index = jnp.arange(count, dtype=jnp.int32)
    same = (owned[:, None] == owned[None, :]) & (index[None, :] < index[:, None])
    return (owned, jnp.sum(same.astype(jnp.int32), axis=1))


def route(states, owned, rank):
    prompt_batch = states.shape[0]
    owners_count = lax.axis_size("dec")
    pairs = (prompt_batch + owners_count - 1) // owners_count
    picks = jnp.arange(pairs, dtype=jnp.int32)
    whole = lax.all_gather(states, "dec", axis=1, tiled=True)
    mine = lax.axis_index("dec")
    select = ((owned[None, :] == mine) & (rank[None, :] == picks[:, None])).astype(jnp.float32)
    picked = jnp.einsum("jr,rhcd->jhcd", select, whole, precision=lax.Precision.HIGHEST)
    return lax.all_to_all(picked, "pre", split_axis=1, concat_axis=0, tiled=True)


def shards(queries, keys, values, log_decay, prior_state, lengths, owners):
    live, total = decay_sums(log_decay, lengths)
    owned, rank = owner_rank(owners)
    prefill_out = span_output(queries, keys, values, prior_state, live, total)
    states = span_state(keys, values, prior_state, live, total)
    decode_state = route(states, owned, rank)
    return (prefill_out, decode_state)


def solution(mesh):
    placed = (
        P(("rep", "pre"), None, "dec"),
        P(("rep", "pre"), None, "dec"),
        P(("rep", "pre"), None, "dec"),
        P(("rep", "pre"), None, "dec"),
        P(("rep", "pre"), "dec", None, None),
        P(("rep", "pre")),
        P(("rep", "pre"), None),
    )
    return jax.shard_map(
        shards,
        mesh=mesh,
        in_specs=placed,
        out_specs=(P(("rep", "pre"), None, "dec"), P(("rep", "dec"), "pre", None, None)),
        check_vma=False,
    )
```

profile of v0, /device:TPU:2, one launch (start us, length us, event | category | flops | bytes accessed | tf_op | source)
XLA Modules:
  0.0 339.8 jit_solution(7889281845861623298)
XLA Ops:
  7.2 0.0 copy-start
  7.2 0.0 all-gather.2.cloned.1.call-start
  7.2 0.8 fusion.27
  8.1 0.7 multiply_bitcast_fusion
  8.8 7.2 %reduce-window.6 = f32[6,4,2,128]{3,2,1,0:T(2,128)S(1)} reduce-window(f32[6,4,2,128]{3,2,1,0:T(2,128)S(1)} %reshape.141, f32[]{:T(128)} %constant.5.clone.1), window={size=1x1x1x128 pad=0_0x0_0x0_0x127_0}, to_apply=%region_0.0 | reduce-window | flops 780288 | bytes 49156 | tf_op jit(solution)/shard_map/reduce-window
  16.1 0.1 slice.12
  16.2 0.1 copy.31
  16.3 0.1 copy.32
  16.4 0.1 broadcast_add_fusion
  16.6 0.1 slice.14
  16.6 0.1 copy.36
  16.8 0.1 copy.39
  16.9 0.1 exponential_multiply_fusion
  17.0 1.7 copy.46
  18.7 0.1 copy.37
  18.8 3.6 %multiply_add_fusion = f32[6,4,128,128]{3,2,1,0:T(8,128)} fusion(f32[6,4,128,128]{3,2,1,0:T(8,128)} %param.11, bf16[6,256,4,128]{1,3,2,0:T(8,128)(2,1)S(1)} %bitcast.67, f32[6,256,4]{1,2,0:T(4,128)S(1)} %get-tuple-element.8, f32[6,4]{1,0:T(8,128)S(1)} %copy.37, bf16[6,256,512]{2,1,0:T(8,128)(2,1)} %param.9), kind=kOutput, calls=%fused_computation.21 | convolution fusion | flops 204472320 | bytes 6316128 | tf_op jit(solution)/shard_map/lmkw,lmkf->lkwf/dot_general | solution.py:49
  22.4 0.0 copy-start.1
  22.4 0.0 all-gather.2.cloned.1.call-update
  22.4 0.6 copy-done.1
  23.0 0.2 convert_reduce_fusion
  23.2 161.5 %all-gather.2.cloned.1.call-done = f32[6,64,128,128]{3,2,1,0:T(8,128)} async-done(((f32[6,4,128,128]{3,2,1,0:T(8,128)}), f32[6,64,128,128]{3,2,1,0:T(8,128)}) %all-gather.2.cloned.1.call-update) | async-done | bytes 25165840 | tf_op jit(solution)/shard_map/all_gather | solution.py:68
  184.7 40.2 %fusion = f32[1,64,128,128]{3,0,2,1:T(1,128)} fusion(f32[6,64,128,128]{3,2,1,0:T(8,128)} %all-gather.2.cloned.1.call-done, s32[6]{0:T(128)S(1)} %convert_reduce_fusion, s32[]{:T(128)S(6)} %axis_index.15, s32[6,1]{0,1:T(1,128)S(1)} %copy-done.1), kind=kOutput, calls=%fused_computation | convolution fusion | flops 75497488 | bytes 29360180 | tf_op jit(solution)/shard_map/jr,rhcd->jhcd/dot_general | solution.py:71
  224.9 7.0 %all-to-all-start = ((f32[1,64,128,128]{3,2,0,1:T(8,128)}), f32[1,64,128,128]{3,2,0,1:T(8,128)}, u32[]{:S(2)}, u32[]{:S(2)}) async-start(f32[1,64,128,128]{3,2,0,1:T(8,128)} %bitcast.66), calls=%async_computation | async-start | bytes 8388608 | tf_op jit(solution)/shard_map/all_to_all | solution.py:72
  231.9 0.0 copy-done
  231.9 5.0 %fusion.2 = f32[6,4,256,128]{2,3,1,0:T(8,128)} fusion(f32[6,256]{1,0:T(8,128)S(1)} %fusion.27, f32[6,4,256]{2,1,0:T(4,128)S(1)} %reduce_window_sum.24, pred[256,256]{1,0:T(8,128)(4,1)S(1)} %iota_compare_fusion, bf16[6,256,4,128]{1,3,2,0:T(8,128)(2,1)S(1)} %bitcast.68, bf16[6,256,512]{2,1,0:T(8,128)(2,1)} %param.9, bf16[6,256,512]{2,1,0:T(8,128)(2,1)S(1)} %copy-done), kind=kOutput, calls=%fused_computation.3 | convolution fusion | flops 813170688 | bytes 7960576 | tf_op jit(solution)/shard_map/fijv,fvil->fjil/dot_general | solution.py:29
  236.9 4.1 %fusion.5 = bf16[6,256,4,128]{1,3,2,0:T(8,128)(2,1)S(1)} fusion(f32[6,4,256,128]{2,3,1,0:T(8,128)} %fusion.2, f32[6,4,128,128]{3,2,1,0:T(8,128)} %param.11, f32[6,256]{1,0:T(8,128)S(1)} %fusion.27, f32[6,256,4]{1,2,0:T(4,128)S(1)} %get-tuple-element.9, bf16[6,256,512]{2,1,0:T(8,128)(2,1)S(1)} %copy-done), kind=kOutput, calls=%fused_computation.7 | convolution fusion | flops 1211105280 | bytes 7895040 | tf_op jit(solution)/shard_map/rthc,rhcd->rthd/dot_general | solution.py:32
  241.0 1.6 copy.41
  242.6 85.7 %all-to-all-done = f32[1,64,128,128]{3,2,0,1:T(8,128)} async-done(((f32[1,64,128,128]{3,2,0,1:T(8,128)}), f32[1,64,128,128]{3,2,0,1:T(8,128)}, u32[]{:S(2)}, u32[]{:S(2)}) %all-to-all-start) | async-done | bytes 4194336 | tf_op jit(solution)/shard_map/all_to_all | solution.py:72
  328.3 4.7 %copy.69 = f32[8,8,128,128]{3,2,1,0:T(8,128)} copy(f32[8,8,128,128]{3,2,1,0:T(8,128)} %bitcast.13) | data formatting | bytes 8388608
  (6 shorter events, 0.1 us)
Async XLA Ops:
  7.2 224.8 %copy-start = (bf16[6,256,512]{2,1,0:T(8,128)(2,1)S(1)}, bf16[6,256,512]{2,1,0:T(8,128)(2,1)}, u32[]{:S(2)}) copy-start(bf16[6,256,512]{2,1,0:T(8,128)(2,1)} %param.7) | copy-start | bytes 4718596
  7.2 177.5 %all-gather.2.cloned.1.call-start = ((), (), s32[]{:S(2)}) async-start(), calls=%async_computation.1 | async-start | bytes 26738688 | tf_op jit(solution)/shard_map/all_gather | solution.py:68
  22.4 0.7 copy-start.1
  224.9 103.4 %all-to-all-start = ((f32[1,64,128,128]{3,2,0,1:T(8,128)}), f32[1,64,128,128]{3,2,0,1:T(8,128)}, u32[]{:S(2)}, u32[]{:S(2)}) async-start(f32[1,64,128,128]{3,2,0,1:T(8,128)} %bitcast.66), calls=%async_computation | async-start | bytes 8388608 | tf_op jit(solution)/shard_map/all_to_all | solution.py:72
Sparse Core Ops, SparseCore 0:
  22.5 162.1 all-gather.1
where the time goes:
time: 341 us; the launch traced here: 340 us
  waiting for transfers between devices  247 us (72%)
  matrix products  52.9 us (16%)
  between operations  14.1 us (4%)
  local copies, waits for them, and re-layouts  9.39 us (3%)
  other arithmetic  9.22 us (3%)
  starting transfers between devices  7.04 us (2%)
    all_gather x1, waiting for transfers between devices, route(): whole = lax.all_gather(states, 'dec', axis=1, tiled=True)  161 us
    all_to_all x1, waiting for transfers between devices, route(): lax.all_to_all(picked, 'pre', split_axis=1, concat_axis=0, tiled=True)  85.7 us
    dot_general x1, matrix products, route(): jnp.einsum('jr,rhcd->jhcd', select, whole, precision=lax.Precision.HIGHEST)  40.2 us
    another operation x3, other arithmetic  7.34 us
    all_to_all x1, starting transfers between devices, route(): lax.all_to_all(picked, 'pre', split_axis=1, concat_axis=0, tiled=True)  7.01 us
    unnamed x6, local copies, waits for them, and re-layouts  6.91 us
  transfers between devices with their start and end apart: 2, of which 2 were waited for; matrix products, arithmetic and copies ran while one was open for 3% of the time, Pallas kernels for 0%

commit v1 on v0

v1 whole, which is shorter than its diff:
```python
import jax
import jax.numpy as jnp
from jax import lax
from jax.experimental import pallas as pl
from jax.experimental.pallas import tpu as pltpu
from jax.sharding import PartitionSpec as P

HD = 128
ROWS = 8


def head_of(h):
    return slice(h * HD, (h + 1) * HD)


def column_sums(rate_rows):
    tokens = rate_rows.shape[1]
    row = lax.broadcasted_iota(jnp.int32, (tokens, tokens), 0)
    col = lax.broadcasted_iota(jnp.int32, (tokens, tokens), 1)
    lower = (col <= row).astype(jnp.float32)
    return lax.dot_general(
        lower, rate_rows, (((1,), (1,)), ((), ())),
        precision=lax.Precision.HIGHEST, preferred_element_type=jnp.float32,
    )


def row_sums(rate_rows):
    tokens = rate_rows.shape[1]
    row = lax.broadcasted_iota(jnp.int32, (tokens, tokens), 0)
    col = lax.broadcasted_iota(jnp.int32, (tokens, tokens), 1)
    upper = (row <= col).astype(jnp.float32)
    return lax.dot_general(
        rate_rows, upper, (((1,), (0,)), ((), ())),
        precision=lax.Precision.HIGHEST, preferred_element_type=jnp.float32,
    )


def state_kernel(lengths_ref, k_ref, v_ref, ld_ref, prior_ref, *out_refs):
    r = pl.program_id(0)
    length = lengths_ref[r]
    heads, tokens = ld_ref.shape[1:]
    per = heads // len(out_refs)
    live_row = lax.broadcasted_iota(jnp.int32, (heads, tokens), 1) < length
    total = column_sums(jnp.where(live_row, ld_ref[0], 0.0))
    last = total[tokens - 1:tokens, :]
    live_col = lax.broadcasted_iota(jnp.int32, (tokens, heads), 0) < length
    keep = jnp.where(live_col, jnp.exp(last - total), 0.0)
    final = jnp.exp(last)
    for h in range(heads):
        k = k_ref[0, :, head_of(h)].astype(jnp.float32)
        decayed = (k * keep[:, h:h + 1]).astype(jnp.bfloat16)
        fresh = lax.dot_general(
            decayed, v_ref[0, :, head_of(h)], (((0,), (0,)), ((), ())),
            preferred_element_type=jnp.float32,
        )
        state = final[:, h:h + 1] * prior_ref[0, h] + fresh
        out_refs[h // per][:, 0, h % per] = state.reshape(HD // ROWS, ROWS, HD)


def span_states(lengths, keys, values, ld, prior, chunks):
    prompts, tokens, width = keys.shape
    heads = ld.shape[1]
    per = heads // chunks
    pieces = HD // ROWS
    return pl.pallas_call(
        state_kernel,
        grid_spec=pltpu.PrefetchScalarGridSpec(
            num_scalar_prefetch=1,
            grid=(prompts,),
            in_specs=[
                pl.BlockSpec((1, tokens, width), lambda r, s: (r, 0, 0)),
                pl.BlockSpec((1, tokens, width), lambda r, s: (r, 0, 0)),
                pl.BlockSpec((1, heads, tokens), lambda r, s: (r, 0, 0)),
                pl.BlockSpec((1, heads, HD, HD), lambda r, s: (r, 0, 0, 0)),
            ],
            out_specs=[
                pl.BlockSpec((pieces, 1, per, ROWS, HD), lambda r, s: (0, r, 0, 0, 0))
                for _ in range(chunks)
            ],
        ),
        out_shape=[
            jax.ShapeDtypeStruct((pieces, prompts, per, ROWS, HD), jnp.float32)
            for _ in range(chunks)
        ],
        compiler_params=pltpu.CompilerParams(vmem_limit_bytes=32 << 20),
        name="span_states",
    )(lengths, keys, values, ld, prior)


def output_kernel(lengths_ref, q_ref, k_ref, v_ref, ld_ref, prior_ref, out_ref):
    r = pl.program_id(0)
    length = lengths_ref[r]
    heads, tokens = ld_ref.shape[1:]
    live_row = lax.broadcasted_iota(jnp.int32, (heads, tokens), 1) < length
    rate = jnp.where(live_row, ld_ref[0], 0.0)
    total_col = column_sums(rate)
    total_row = row_sums(rate)
    grow = jnp.exp(total_col)
    row = lax.broadcasted_iota(jnp.int32, (tokens, tokens), 0)
    col = lax.broadcasted_iota(jnp.int32, (tokens, tokens), 1)
    seen = (col <= row) & (col < length)
    live_col = lax.broadcasted_iota(jnp.int32, (tokens, HD), 0) < length
    for h in range(heads):
        q = q_ref[0, :, head_of(h)]
        score = lax.dot_general(
            q, k_ref[0, :, head_of(h)], (((1,), (1,)), ((), ())),
            preferred_element_type=jnp.float32,
        )
        gap = jnp.where(seen, total_col[:, h:h + 1] - total_row[h:h + 1, :], -jnp.inf)
        weight = (score * jnp.exp(gap)).astype(jnp.bfloat16)
        inner = jnp.dot(weight, v_ref[0, :, head_of(h)], preferred_element_type=jnp.float32)
        prior = prior_ref[0, h]
        high = prior.astype(jnp.bfloat16)
        rest = prior - high.astype(jnp.float32)
        mid = rest.astype(jnp.bfloat16)
        low = (rest - mid.astype(jnp.float32)).astype(jnp.bfloat16)
        carried = jnp.dot(q, low, preferred_element_type=jnp.float32)
        carried = carried + jnp.dot(q, mid, preferred_element_type=jnp.float32)
        carried = carried + jnp.dot(q, high, preferred_element_type=jnp.float32)
        out = inner + carried * grow[:, h:h + 1]
        out_ref[0, :, head_of(h)] = jnp.where(live_col, out, 0.0).astype(jnp.bfloat16)


def span_output(lengths, queries, keys, values, ld, prior):
    prompts, tokens, width = keys.shape
    heads = ld.shape[1]
    span = pl.BlockSpec((1, tokens, width), lambda r, s: (r, 0, 0))
    return pl.pallas_call(
        output_kernel,
        grid_spec=pltpu.PrefetchScalarGridSpec(
            num_scalar_prefetch=1,
            grid=(prompts,),
            in_specs=[
                span, span, span,
                pl.BlockSpec((1, heads, tokens), lambda r, s: (r, 0, 0)),
                pl.BlockSpec((1, heads, HD, HD), lambda r, s: (r, 0, 0, 0)),
            ],
            out_specs=span,
        ),
        out_shape=jax.ShapeDtypeStruct((prompts, tokens, width), jnp.bfloat16),
        compiler_params=pltpu.CompilerParams(vmem_limit_bytes=32 << 20),
        cost_estimate=pl.CostEstimate(
            flops=2 * prompts * heads * tokens * HD * (2 * tokens + 3 * HD),
            bytes_accessed=8 * prompts * tokens * width + 4 * prompts * heads * HD * HD,
            transcendentals=prompts * heads * tokens * tokens,
        ),
        name="span_output",
    )(lengths, queries, keys, values, ld, prior)


def address_kernel(owners_ref, held_ref, out_ref, sem):
    groups, _, prompts = held_ref.shape[:3]

    def block(i):
        g = i // prompts
        r = i % prompts
        return pltpu.make_async_copy(
            held_ref.at[g, :, r], out_ref.at[owners_ref[i], g], sem
        )

    @pl.loop(0, groups * prompts)
    def _(i):
        block(i).start()

    pltpu.make_async_copy(held_ref, held_ref, sem).wait()


def address(all_owners, held, count):
    groups, halves, prompts, per = held.shape[:4]
    return pl.pallas_call(
        address_kernel,
        in_specs=[
            pl.BlockSpec(memory_space=pltpu.SMEM),
            pl.BlockSpec(memory_space=pl.ANY),
        ],
        out_specs=pl.BlockSpec(memory_space=pl.ANY),
        out_shape=jax.ShapeDtypeStruct((count, groups, halves, per, ROWS, HD), jnp.float32),
        scratch_shapes=[pltpu.SemaphoreType.DMA],
        name="address",
    )(all_owners, held)


def place_kernel(present_ref, *refs):
    out_ref = refs[-1]
    g = pl.program_id(0)
    here = present_ref[g] > 0
    chunks = len(refs) - 1

    @pl.when(here)
    def _():
        for c in range(chunks):
            pieces, _, halves, per = refs[c].shape[:4]
            for b in range(halves):
                for e in range(per):
                    h = (b * chunks + c) * per + e
                    out_ref[0, h] = refs[c][:, 0, b, e].reshape(pieces * ROWS, HD)

    @pl.when(jnp.logical_not(here))
    def _():
        out_ref[...] = jnp.zeros_like(out_ref)


def place(present, parts):
    pieces, groups, halves, per = parts[0].shape[:4]
    heads = halves * per * len(parts)
    return pl.pallas_call(
        place_kernel,
        grid_spec=pltpu.PrefetchScalarGridSpec(
            num_scalar_prefetch=1,
            grid=(groups,),
            in_specs=[
                pl.BlockSpec((pieces, 1, halves, per, ROWS, HD), lambda g, s: (0, g, 0, 0, 0, 0))
                for _ in parts
            ],
            out_specs=pl.BlockSpec((1, heads, HD, HD), lambda g, s: (g, 0, 0, 0)),
        ),
        out_shape=jax.ShapeDtypeStruct((groups, heads, HD, HD), jnp.float32),
        compiler_params=pltpu.CompilerParams(vmem_limit_bytes=32 << 20),
        name="place",
    )(present, *parts)


CHUNKS = 1


def shards(queries, keys, values, log_decay, prior_state, lengths, owners):
    n_pre = lax.axis_size("pre")
    n_dec = lax.axis_size("dec")
    prompts = keys.shape[0]
    ld = jnp.swapaxes(log_decay, 1, 2)
    all_owners = lax.all_gather(owners[:, 0], "pre", axis=0, tiled=True)
    mine = lax.axis_index("dec")
    present = jnp.any(all_owners.reshape(n_pre, prompts) == mine, axis=1).astype(jnp.int32)
    states = span_states(lengths, keys, values, ld, prior_state, CHUNKS)
    parts = []
    for piece in states:
        mixed = lax.all_to_all(piece, "dec", split_axis=0, concat_axis=0, tiled=True)
        held = lax.all_to_all(mixed, "pre", split_axis=0, concat_axis=0, tiled=True)
        held = held.reshape((n_pre, n_dec // n_pre) + held.shape[1:])
        sent = address(all_owners, held, n_dec)
        parts.append(lax.all_to_all(sent, "dec", split_axis=0, concat_axis=0, tiled=True))
    prefill_out = span_output(lengths, queries, keys, values, ld, prior_state)
    decode_state = place(present, parts)
    return prefill_out, decode_state


def solution(mesh):
    placed = (
        P(("rep", "pre"), None, "dec"),
        P(("rep", "pre"), None, "dec"),
        P(("rep", "pre"), None, "dec"),
        P(("rep", "pre"), None, "dec"),
        P(("rep", "pre"), "dec", None, None),
        P(("rep", "pre")),
        P(("rep", "pre"), None),
    )
    return jax.shard_map(
        shards,
        mesh=mesh,
        in_specs=placed,
        out_specs=(P(("rep", "pre"), None, "dec"), P(("rep", "dec"), "pre", None, None)),
        check_vma=False,
    )
```

time: 341 us -> 217 us (0.64)
  the two profiles are of different devices: /device:TPU:2 before, /device:TPU:96 now
where the time goes in v1:
time: 217 us; the launch traced here: 216 us
  blocking collectives  71.5 us (33%)
  Pallas kernels  70.8 us (33%)
  waiting for transfers between devices  49 us (23%)
  starting transfers between devices  12.6 us (6%)
  local copies, waits for them, and re-layouts  10.4 us (5%)
    pallas_call x1, Pallas kernels, address(): pl.pallas_call(address_kernel, in_specs=[pl.BlockSpec(memory_space=pltpu....  49.4 us
    all_to_all x1, waiting for transfers between devices, shards(): lax.all_to_all(sent, 'dec', split_axis=0, concat_axis=0, tiled=True)  49 us
    all_gather x1, blocking collectives, shards(): all_owners = lax.all_gather(owners[:, 0], 'pre', axis=0, tiled=True)  41.8 us
    all_to_all x1, blocking collectives, shards(): lax.all_to_all(piece, 'dec', split_axis=0, concat_axis=0, tiled=True)  29.7 us
    unnamed x33, local copies, waits for them, and re-layouts  10.3 us
    pallas_call x1, Pallas kernels, span_output(): pl.pallas_call(output_kernel, grid_spec=pltpu.PrefetchScalarGridSpec(num_...  8.18 us
    all_to_all x1, starting transfers between devices, shards(): held = lax.all_to_all(mixed, 'pre', split_axis=0, concat_axis=0, tiled=True)  7.79 us
    pallas_call x1, Pallas kernels, place(): pl.pallas_call(place_kernel, grid_spec=pltpu.PrefetchScalarGridSpec(num_s...  7.16 us
  transfers between devices with their start and end apart: 2, of which 1 were waited for; matrix products, arithmetic and copies ran while one was open for 0% of the time, Pallas kernels for 4%

profile of v1, /device:TPU:96, one launch (start us, length us, event | category | flops | bytes accessed | tf_op | source)
XLA Modules:
  0.0 215.9 jit_solution(9600547970005079723)
XLA Ops:
  0.6 0.0 copy-start
  0.6 1.4 copy-done
  2.0 0.0 copy-start.2
  2.0 1.4 copy-done.2
  3.4 0.0 copy-start.4
  3.5 1.4 copy-done.4
  4.9 0.0 copy-start.7
  4.9 0.7 copy-done.7
  5.6 0.0 copy-start.9
  5.6 0.7 copy-done.9
  6.3 6.0 %span_states.1 = f32[16,6,4,8,128]{4,3,2,1,0:T(8,128)S(1)} custom-call(s32[6]{0:T(128)S(1)} %copy-done.9, bf16[6,256,512]{2,1,0:T(8,128)(2,1)S(1)} %copy-done, bf16[6,256,512]{2,1,0:T(8,128)(2,1)S(1)} %copy-done.2, f32[6,4,256]{2,1,0:T(4,128)S(1)} %bitcast.5, f32[6,4,128,128]{3,2,1,0:T(8,128)S(1)} %copy-done.4), custom_call_target="tpu_custom_call" | custom-call | tf_op jit(solution)/shard_map/span_states/pallas_call | solution.py:65
  12.3 29.7 %all_to_all.15 = f32[16,6,4,8,128]{4,3,2,1,0:T(8,128)} all-to-all(f32[16,6,4,8,128]{4,3,2,1,0:T(8,128)S(1)} %span_states.1), channel_id=1, replica_groups=mesh['pre'=8,'dec'=16,'rep'=2] {'dec'}, dimensions={0} | all-to-all | bytes 3145728 | tf_op jit(solution)/shard_map/all_to_all | solution.py:237
  42.0 0.0 copy-start.14
  42.0 0.0 copy-start.13
  42.0 7.8 %all-to-all-start.1 = ((f32[16,6,4,8,128]{4,3,2,1,0:T(8,128)}), f32[16,6,4,8,128]{4,3,2,1,0:T(8,128)S(1)}, u32[]{:S(2)}, u32[]{:S(2)}) async-start(f32[16,6,4,8,128]{4,3,2,1,0:T(8,128)} %all_to_all.15), calls=%async_computation.1 | async-start | bytes 3145728 | tf_op jit(solution)/shard_map/all_to_all | solution.py:238
  49.8 0.0 copy-done.14
  49.8 0.6 dynamic-slice
  51.1 0.0 copy-done.13
  51.1 0.1 bitcast_dynamic-update-slice_fusion
  51.2 41.8 %all-reduce.owners_ref = s32[48]{0:T(128)} all-reduce(s32[48]{0:T(128)S(1)} %bitcast_dynamic-update-slice_fusion), channel_id=2, replica_groups=mesh['pre'=8,'dec'=16,'rep'=2] {'pre'}, use_global_device_ids=true, to_apply=%add | all-reduce | flops 48 | bytes 384 | tf_op jit(solution)/shard_map/all_gather | solution.py:231
  93.0 0.0 all-to-all-done.1
  93.0 0.0 copy-start.11
  93.0 1.1 copy-done.11
  94.1 49.4 %address.1 = f32[16,8,2,4,8,128]{5,4,3,2,1,0:T(8,128)} custom-call(s32[48]{0:T(128)} %all-reduce.owners_ref, f32[8,2,6,4,8,128]{5,4,3,2,1,0:T(8,128)} %bitcast.7), custom_call_target="tpu_custom_call" | custom-call | tf_op jit(solution)/shard_map/address/pallas_call | solution.py:170
  143.5 0.0 copy-start.12
  143.6 0.0 copy-start.1
  143.6 0.0 copy-start.3
  143.6 0.0 copy-start.8
  143.6 0.0 copy-start.10
  143.6 4.8 %all-to-all-start.2 = ((f32[16,8,2,4,8,128]{5,4,3,2,1,0:T(8,128)}), f32[16,8,2,4,8,128]{5,4,3,2,1,0:T(8,128)}, u32[]{:S(2)}, u32[]{:S(2)}) async-start(f32[16,8,2,4,8,128]{5,4,3,2,1,0:T(8,128)} %address.1), calls=%async_computation.2 | async-start | bytes 8388608 | tf_op jit(solution)/shard_map/all_to_all | solution.py:241
  148.4 0.0 copy-done.12
  148.5 0.1 eq.11
  148.5 0.1 reduce_or.9
  148.7 0.0 copy-done.1
  148.7 0.0 copy-done.3
  148.7 0.0 copy-done.8
  148.7 0.0 copy-done.10
  148.7 0.0 copy-start.5
  148.7 1.4 copy-done.5
  150.1 0.0 copy-start.6
  150.1 1.4 copy-done.6
  151.5 8.2 %span_output.1 = bf16[6,256,512]{2,1,0:T(8,128)(2,1)} custom-call(s32[6]{0:T(128)S(1)} %copy-done.10, bf16[6,256,512]{2,1,0:T(8,128)(2,1)S(1)} %copy-done.6, bf16[6,256,512]{2,1,0:T(8,128)(2,1)S(1)} %copy-done.1, bf16[6,256,512]{2,1,0:T(8,128)(2,1)S(1)} %copy-done.3, f32[6,4,256]{2,1,0:T(4,128)S(1)} %bitcast.6, f32[6,4,128,128]{3,2,1,0:T(8,128)S(1)} %copy-done.5), custom_call_target="tpu_custom_call" | custom-call | flops 1409286144 | bytes 7864320 | tf_op jit(solution)/shard_map/span_output/pallas_call | solution.py:128
  159.7 49.0 %all-to-all-done.2.refs_0_ = f32[16,8,2,4,8,128]{5,4,3,2,1,0:T(8,128)} async-done(((f32[16,8,2,4,8,128]{5,4,3,2,1,0:T(8,128)}), f32[16,8,2,4,8,128]{5,4,3,2,1,0:T(8,128)}, u32[]{:S(2)}, u32[]{:S(2)}) %all-to-all-start.2) | async-done | bytes 4194336 | tf_op jit(solution)/shard_map/all_to_all | solution.py:241
  208.7 7.2 %place.1 = f32[8,8,128,128]{3,2,1,0:T(8,128)} custom-call(s32[8]{0:T(128)S(1)} %convert_element_type.3.present_ref, f32[16,8,2,4,8,128]{5,4,3,2,1,0:T(8,128)} %all-to-all-done.2.refs_0_), custom_call_target="tpu_custom_call" | custom-call | tf_op jit(solution)/shard_map/place/pallas_call | solution.py:206
  (3 shorter events, 0.0 us)
Async XLA Ops:
  0.6 1.4 copy-start
  2.0 1.4 copy-start.2
  3.4 1.4 copy-start.4
  4.9 0.7 copy-start.7
  5.6 0.7 copy-start.9
  42.0 7.8 %copy-start.14 = (u32[256]{0:T(256)S(1)}, u32[256]{0:T(256)}, u32[]{:S(2)}) copy-start(u32[256]{0:T(256)} %constant.17) | copy-start | bytes 3076
  42.0 9.0 %copy-start.13 = (s32[6,1]{0,1:T(1,128)S(1)}, s32[6,1]{0,1:T(1,128)}, u32[]{:S(2)}) copy-start(s32[6,1]{0,1:T(1,128)} %param.13) | copy-start | bytes 76
  42.0 51.0 %all-to-all-start.1 = ((f32[16,6,4,8,128]{4,3,2,1,0:T(8,128)}), f32[16,6,4,8,128]{4,3,2,1,0:T(8,128)S(1)}, u32[]{:S(2)}, u32[]{:S(2)}) async-start(f32[16,6,4,8,128]{4,3,2,1,0:T(8,128)} %all_to_all.15), calls=%async_computation.1 | async-start | bytes 3145728 | tf_op jit(solution)/shard_map/all_to_all | solution.py:238
  93.0 1.1 copy-start.11
  143.5 4.9 %copy-start.12 = (s32[48]{0:T(128)S(1)}, s32[48]{0:T(128)}, u32[]{:S(2)}) copy-start(s32[48]{0:T(128)} %all-reduce.owners_ref) | copy-start | bytes 580
  143.6 5.1 %copy-start.1 = (bf16[6,256,512]{2,1,0:T(8,128)(2,1)S(1)}, bf16[6,256,512]{2,1,0:T(8,128)(2,1)}, u32[]{:S(2)}) copy-start(bf16[6,256,512]{2,1,0:T(8,128)(2,1)} %k_ref.3) | copy-start | bytes 4718596
  143.6 5.1 %copy-start.3 = (bf16[6,256,512]{2,1,0:T(8,128)(2,1)S(1)}, bf16[6,256,512]{2,1,0:T(8,128)(2,1)}, u32[]{:S(2)}) copy-start(bf16[6,256,512]{2,1,0:T(8,128)(2,1)} %v_ref.3) | copy-start | bytes 4718596
  143.6 5.1 %copy-start.8 = (f32[6,256,4]{1,2,0:T(4,128)S(1)}, f32[6,256,4]{1,2,0:T(4,128)}, u32[]{:S(2)}) copy-start(f32[6,256,4]{1,2,0:T(4,128)} %param.10) | copy-start | bytes 73732
  143.6 5.1 %copy-start.10 = (s32[6]{0:T(128)S(1)}, s32[6]{0:T(128)}, u32[]{:S(2)}) copy-start(s32[6]{0:T(128)} %lengths_ref.3) | copy-start | bytes 76
  143.6 65.1 %all-to-all-start.2 = ((f32[16,8,2,4,8,128]{5,4,3,2,1,0:T(8,128)}), f32[16,8,2,4,8,128]{5,4,3,2,1,0:T(8,128)}, u32[]{:S(2)}, u32[]{:S(2)}) async-start(f32[16,8,2,4,8,128]{5,4,3,2,1,0:T(8,128)} %address.1), calls=%async_computation.2 | async-start | bytes 8388608 | tf_op jit(solution)/shard_map/all_to_all | solution.py:241
  148.7 1.4 copy-start.5
  150.1 1.4 copy-start.6

commit v2 on v1

--- a/solution.py
+++ b/solution.py
@@ -1,3 +1,5 @@
+import functools
+
 import jax
 import jax.numpy as jnp
 from jax import lax
@@ -7,6 +9,8 @@
 
 HD = 128
 ROWS = 8
+VMEM = 56 << 20
+SHIFTS = ((0, 1, 7, 2), (6, 3, 5, 4))
 
 
 def head_of(h):
@@ -35,11 +39,10 @@
     )
 
 
-def state_kernel(lengths_ref, k_ref, v_ref, ld_ref, prior_ref, *out_refs):
+def state_kernel(lengths_ref, k_ref, v_ref, ld_ref, prior_ref, owners_ref, out_ref):
     r = pl.program_id(0)
     length = lengths_ref[r]
     heads, tokens = ld_ref.shape[1:]
-    per = heads // len(out_refs)
     live_row = lax.broadcasted_iota(jnp.int32, (heads, tokens), 1) < length
     total = column_sums(jnp.where(live_row, ld_ref[0], 0.0))
     last = total[tokens - 1:tokens, :]
@@ -54,14 +57,21 @@
             preferred_element_type=jnp.float32,
         )
         state = final[:, h:h + 1] * prior_ref[0, h] + fresh
-        out_refs[h // per][:, 0, h % per] = state.reshape(HD // ROWS, ROWS, HD)
-
-
-def span_states(lengths, keys, values, ld, prior, chunks):
+        out_ref[:, r * heads + h] = state.reshape(HD // ROWS, ROWS, HD)
+
+    @pl.when(r == 0)
+    def _():
+        named = jnp.broadcast_to(owners_ref[...], out_ref.shape[2:])
+        for j in range(out_ref.shape[0]):
+            out_ref[j, out_ref.shape[1] - 1] = named
+
+
+def span_states(lengths, keys, values, ld, prior, owners):
     prompts, tokens, width = keys.shape
     heads = ld.shape[1]
-    per = heads // chunks
     pieces = HD // ROWS
+    named = jnp.pad(owners.astype(jnp.float32), ((0, ROWS - prompts), (0, 0)))
+    shape = (pieces, prompts * heads + 1, ROWS, HD)
     return pl.pallas_call(
         state_kernel,
         grid_spec=pltpu.PrefetchScalarGridSpec(
@@ -72,19 +82,14 @@
                 pl.BlockSpec((1, tokens, width), lambda r, s: (r, 0, 0)),
                 pl.BlockSpec((1, heads, tokens), lambda r, s: (r, 0, 0)),
                 pl.BlockSpec((1, heads, HD, HD), lambda r, s: (r, 0, 0, 0)),
+                pl.BlockSpec((ROWS, 1), lambda r, s: (0, 0)),
             ],
-            out_specs=[
-                pl.BlockSpec((pieces, 1, per, ROWS, HD), lambda r, s: (0, r, 0, 0, 0))
-                for _ in range(chunks)
-            ],
+            out_specs=pl.BlockSpec(shape, lambda r, s: (0, 0, 0, 0)),
         ),
-        out_shape=[
-            jax.ShapeDtypeStruct((pieces, prompts, per, ROWS, HD), jnp.float32)
-            for _ in range(chunks)
-        ],
-        compiler_params=pltpu.CompilerParams(vmem_limit_bytes=32 << 20),
+        out_shape=jax.ShapeDtypeStruct(shape, jnp.float32),
+        compiler_params=pltpu.CompilerParams(vmem_limit_bytes=VMEM),
         name="span_states",
-    )(lengths, keys, values, ld, prior)
+    )(lengths, keys, values, ld, prior, named)
 
 
 def output_kernel(lengths_ref, q_ref, k_ref, v_ref, ld_ref, prior_ref, out_ref):
@@ -138,7 +143,7 @@
             out_specs=span,
         ),
         out_shape=jax.ShapeDtypeStruct((prompts, tokens, width), jnp.bfloat16),
-        compiler_params=pltpu.CompilerParams(vmem_limit_bytes=32 << 20),
+        compiler_params=pltpu.CompilerParams(vmem_limit_bytes=VMEM),
         cost_estimate=pl.CostEstimate(
             flops=2 * prompts * heads * tokens * HD * (2 * tokens + 3 * HD),
             bytes_accessed=8 * prompts * tokens * width + 4 * prompts * heads * HD * HD,
@@ -148,99 +153,126 @@
     )(lengths, queries, keys, values, ld, prior)
 
 
-def address_kernel(owners_ref, held_ref, out_ref, sem):
-    groups, _, prompts = held_ref.shape[:3]
-
-    def block(i):
-        g = i // prompts
-        r = i % prompts
-        return pltpu.make_async_copy(
-            held_ref.at[g, :, r], out_ref.at[owners_ref[i], g], sem
-        )
-
-    @pl.loop(0, groups * prompts)
-    def _(i):
-        block(i).start()
-
-    pltpu.make_async_copy(held_ref, held_ref, sem).wait()
-
-
-def address(all_owners, held, count):
-    groups, halves, prompts, per = held.shape[:4]
-    return pl.pallas_call(
-        address_kernel,
-        in_specs=[
-            pl.BlockSpec(memory_space=pltpu.SMEM),
-            pl.BlockSpec(memory_space=pl.ANY),
+def address_kernel(slots, *refs):
+    held = refs[:slots]
+    out_ref, names, name_sems, sems = refs[slots:]
+    per = out_ref.shape[3]
+    rows = held[0].shape[1] - 1
+    for j in range(slots):
+        pltpu.make_async_copy(held[j].at[0, rows], names.at[j], name_sems.at[j]).start()
+    for j in range(slots):
+        pltpu.make_async_copy(held[j].at[0, rows], names.at[j], name_sems.at[j]).wait()
+        for r in range(rows // per):
+            owner = names[j, r, 0].astype(jnp.int32)
+            pltpu.make_async_copy(
+                held[j].at[:, pl.ds(r * per, per)], out_ref.at[owner, j], sems.at[j]
+            ).start()
+    for j in range(slots):
+        sent = held[j].at[:, pl.ds(0, rows)]
+        pltpu.make_async_copy(sent, sent, sems.at[j]).wait()
+
+
+def address(held, count, heads):
+    slots = len(held)
+    halves = held[0].shape[0]
+    return pl.pallas_call(
+        functools.partial(address_kernel, slots),
+        in_specs=[pl.BlockSpec(memory_space=pltpu.VMEM) for _ in held],
+        out_specs=pl.BlockSpec(memory_space=pl.ANY),
+        out_shape=jax.ShapeDtypeStruct((count, slots, halves, heads, ROWS, HD), jnp.float32),
+        scratch_shapes=[
+            pltpu.SMEM((slots, ROWS, HD), jnp.float32),
+            pltpu.SemaphoreType.DMA((slots,)),
+            pltpu.SemaphoreType.DMA((slots,)),
         ],
-        out_specs=pl.BlockSpec(memory_space=pl.ANY),
-        out_shape=jax.ShapeDtypeStruct((count, groups, halves, per, ROWS, HD), jnp.float32),
-        scratch_shapes=[pltpu.SemaphoreType.DMA],
+        compiler_params=pltpu.CompilerParams(vmem_limit_bytes=VMEM),
         name="address",
-    )(all_owners, held)
-
-
-def place_kernel(present_ref, *refs):
-    out_ref = refs[-1]
-    g = pl.program_id(0)
-    here = present_ref[g] > 0
-    chunks = len(refs) - 1
-
-    @pl.when(here)
-    def _():
-        for c in range(chunks):
-            pieces, _, halves, per = refs[c].shape[:4]
+    )(*held)
+
+
+def place_kernel(groups_ref, present_ref, got_ref, *refs):
+    out_ref, got, placed, in_sems, out_sems = refs[-5:]
+    pieces, slots, halves, per = got_ref.shape[:4]
+
+    def fetch(j):
+        return pltpu.make_async_copy(got_ref.at[:, j], got.at[j], in_sems.at[j])
+
+    def store(j):
+        return pltpu.make_async_copy(placed.at[j], out_ref.at[groups_ref[j]], out_sems.at[j])
+
+    for j in range(slots):
+        @pl.when(present_ref[j] > 0)
+        def _():
+            fetch(j).start()
+
+    for j in range(slots):
+        @pl.when(present_ref[j] == 0)
+        def _():
+            placed[j] = jnp.zeros(placed.shape[1:], jnp.float32)
+
+        @pl.when(present_ref[j] > 0)
+        def _():
+            fetch(j).wait()
             for b in range(halves):
                 for e in range(per):
-                    h = (b * chunks + c) * per + e
-                    out_ref[0, h] = refs[c][:, 0, b, e].reshape(pieces * ROWS, HD)
-
-    @pl.when(jnp.logical_not(here))
-    def _():
-        out_ref[...] = jnp.zeros_like(out_ref)
-
-
-def place(present, parts):
-    pieces, groups, halves, per = parts[0].shape[:4]
-    heads = halves * per * len(parts)
+                    placed[j, b * per + e] = got[j, :, b, e].reshape(pieces * ROWS, HD)
+
+        store(j).start()
+    for j in range(slots):
+        store(j).wait()
+
+
+def place(groups, present, got, n_groups, out=None):
+    pieces, slots, halves, per = got.shape[:4]
+    heads = halves * per
+    smem = pl.BlockSpec(memory_space=pltpu.SMEM)
+    hbm = pl.BlockSpec(memory_space=pl.ANY)
+    given = [groups, present, got] + ([] if out is None else [out])
     return pl.pallas_call(
         place_kernel,
-        grid_spec=pltpu.PrefetchScalarGridSpec(
-            num_scalar_prefetch=1,
-            grid=(groups,),
-            in_specs=[
-                pl.BlockSpec((pieces, 1, halves, per, ROWS, HD), lambda g, s: (0, g, 0, 0, 0, 0))
-                for _ in parts
-            ],
-            out_specs=pl.BlockSpec((1, heads, HD, HD), lambda g, s: (g, 0, 0, 0)),
-        ),
-        out_shape=jax.ShapeDtypeStruct((groups, heads, HD, HD), jnp.float32),
-        compiler_params=pltpu.CompilerParams(vmem_limit_bytes=32 << 20),
+        in_specs=[smem, smem, hbm] + ([] if out is None else [hbm]),
+        out_specs=hbm,
+        out_shape=jax.ShapeDtypeStruct((n_groups, heads, HD, HD), jnp.float32),
+        input_output_aliases={} if out is None else {3: 0},
+        scratch_shapes=[
+            pltpu.VMEM((slots, pieces, halves, per, ROWS, HD), jnp.float32),
+            pltpu.VMEM((slots, heads, HD, HD), jnp.float32),
+            pltpu.SemaphoreType.DMA((slots,)),
+            pltpu.SemaphoreType.DMA((slots,)),
+        ],
+        compiler_params=pltpu.CompilerParams(vmem_limit_bytes=VMEM),
         name="place",
-    )(present, *parts)
-
-
-CHUNKS = 1
+    )(*given)
+
+
+def shifted(mixed, shift, n_pre):
+    halves = mixed.shape[0] // n_pre
+    goal = lax.rem(lax.axis_index("pre") + shift, n_pre)
+    part = lax.dynamic_slice_in_dim(mixed, goal * halves, halves, 0)
+    if shift == 0:
+        return part
+    return lax.ppermute(part, "pre", [(i, (i + shift) % n_pre) for i in range(n_pre)])
 
 
 def shards(queries, keys, values, log_decay, prior_state, lengths, owners):
     n_pre = lax.axis_size("pre")
     n_dec = lax.axis_size("dec")
-    prompts = keys.shape[0]
+    prompts, heads = prior_state.shape[:2]
+    me_pre, me_dec = lax.axis_index("pre"), lax.axis_index("dec")
     ld = jnp.swapaxes(log_decay, 1, 2)
-    all_owners = lax.all_gather(owners[:, 0], "pre", axis=0, tiled=True)
-    mine = lax.axis_index("dec")
-    present = jnp.any(all_owners.reshape(n_pre, prompts) == mine, axis=1).astype(jnp.int32)
-    states = span_states(lengths, keys, values, ld, prior_state, CHUNKS)
-    parts = []
-    for piece in states:
-        mixed = lax.all_to_all(piece, "dec", split_axis=0, concat_axis=0, tiled=True)
-        held = lax.all_to_all(mixed, "pre", split_axis=0, concat_axis=0, tiled=True)
-        held = held.reshape((n_pre, n_dec // n_pre) + held.shape[1:])
-        sent = address(all_owners, held, n_dec)
-        parts.append(lax.all_to_all(sent, "dec", split_axis=0, concat_axis=0, tiled=True))
+    states = span_states(lengths, keys, values, ld, prior_state, owners)
+    mixed = lax.all_to_all(states, "dec", split_axis=0, concat_axis=0, tiled=True)
+    held = {m: shifted(mixed, m, n_pre) for batch in SHIFTS for m in batch}
+    decode_state = None
+    for batch in SHIFTS:
+        blocks = [held[m] for m in batch]
+        sent = address(blocks, n_dec, heads)
+        got = lax.all_to_all(sent, "dec", split_axis=0, concat_axis=0, tiled=True)
+        named = jnp.stack([x[0, -1, :prompts, 0] for x in blocks]).astype(jnp.int32)
+        present = jnp.any(named == me_dec, axis=1).astype(jnp.int32)
+        groups = lax.rem(me_pre + n_pre - jnp.array(batch, jnp.int32), n_pre)
+        decode_state = place(groups, present, got, n_pre, decode_state)
     prefill_out = span_output(lengths, queries, keys, values, ld, prior_state)
-    decode_state = place(present, parts)
     return prefill_out, decode_state
 
 

time: 217 us -> 147 us (0.68)
  blocking collectives: 71.5 us -> 0 us
  Pallas kernels: 70.8 us -> 30.8 us
  starting transfers between devices: 12.6 us -> 35.3 us
  waiting for transfers between devices: 49 us -> 64 us
  other arithmetic: 0.13 us -> 2.45 us
    pallas_call x2 -> x4, Pallas kernels: 56.6 us -> 11.8 us  [the longest x2 6.28 us: place(): pl.pallas_call(place_kernel, in_specs=[smem, smem, hbm] + ([] if out is N...]
    all_gather x1 -> x0, blocking collectives: 41.8 us -> none  [shards(): all_owners = lax.all_gather(owners[:, 0], 'pre', axis=0, tiled=True)]
    ppermute x0 -> x7, waiting for transfers between devices: none -> 33.2 us  [shifted(): lax.ppermute(part, 'pre', [(i, (i + shift) % n_pre) for i in range(n_pre)])]
    all_to_all x1 -> x0, blocking collectives: 29.7 us -> none  [shards(): lax.all_to_all(piece, 'dec', split_axis=0, concat_axis=0, tiled=True)]
    all_to_all x2 -> x3, waiting for transfers between devices: 49 us -> 30.8 us  [the longest x1 25.2 us: shards(): lax.all_to_all(states, 'dec', split_axis=0, concat_axis=0, tiled=True)]
    ppermute x0 -> x7, starting transfers between devices: none -> 16.4 us  [shifted(): lax.ppermute(part, 'pre', [(i, (i + shift) % n_pre) for i in range(n_pre)])]
    slice x0 -> x8, local copies, waits for them, and re-layouts: none -> 6.35 us  [shards(): named = jnp.stack([x[0, -1, :prompts, 0] for x in blocks]).astype(jnp.int32)]
    all_to_all x2 -> x3, starting transfers between devices: 12.6 us -> 18.9 us  [the longest x2 11.8 us: shards(): got = lax.all_to_all(sent, 'dec', split_axis=0, concat_axis=0, tiled=True)]
  transfers between devices with their start and end apart: 2 -> 10, of which waited for: 1 -> 7; matrix products, arithmetic and copies ran while one was open for 0% -> 6% of each run, Pallas kernels for 4% -> 11%
where the time goes in v2:
time: 147 us; the launch traced here: 146 us
  waiting for transfers between devices  64 us (44%)
  starting transfers between devices  35.3 us (24%)
  Pallas kernels  30.8 us (21%)
  local copies, waits for them, and re-layouts  12.4 us (8%)
  other arithmetic  2.45 us (2%)
    ppermute x7, waiting for transfers between devices, shifted(): lax.ppermute(part, 'pre', [(i, (i + shift) % n_pre) for i in range(n_pre)])  33.2 us
    all_to_all x1, waiting for transfers between devices, shards(): lax.all_to_all(states, 'dec', split_axis=0, concat_axis=0, tiled=True)  25.2 us
    ppermute x7, starting transfers between devices, shifted(): lax.ppermute(part, 'pre', [(i, (i + shift) % n_pre) for i in range(n_pre)])  16.4 us
    all_to_all x2, starting transfers between devices, shards(): got = lax.all_to_all(sent, 'dec', split_axis=0, concat_axis=0, tiled=True)  11.8 us
    pallas_call x1, Pallas kernels, span_output(): pl.pallas_call(output_kernel, grid_spec=pltpu.PrefetchScalarGridSpec(num_...  10 us
    pallas_call x1, Pallas kernels, span_states(): pl.pallas_call(state_kernel, grid_spec=pltpu.PrefetchScalarGridSpec(num_s...  8.95 us
    all_to_all x1, starting transfers between devices, shards(): lax.all_to_all(states, 'dec', split_axis=0, concat_axis=0, tiled=True)  7.04 us
    slice x8, local copies, waits for them, and re-layouts, shards(): named = jnp.stack([x[0, -1, :prompts, 0] for x in blocks]).astype(jnp.int32)  6.35 us
  transfers between devices with their start and end apart: 10, of which 7 were waited for; matrix products, arithmetic and copies ran while one was open for 6% of the time, Pallas kernels for 11%

profile of v2, /device:TPU:96, one launch (start us, length us, event | category | flops | bytes accessed | tf_op | source)
XLA Modules:
  0.0 145.8 jit_solution(8932336055019583212)
XLA Ops:
  0.6 0.7 copy.13
  1.4 0.6 pad.4.owners_ref
  2.0 9.0 %span_states.1 = f32[16,25,8,128]{3,2,1,0:T(8,128)} custom-call(s32[6]{0:T(128)} %lengths_ref.3, bf16[6,256,512]{2,1,0:T(8,128)(2,1)} %k_ref.3, bf16[6,256,512]{2,1,0:T(8,128)(2,1)} %v_ref.3, f32[6,4,256]{2,1,0:T(4,128)} %bitcast.9, f32[6,4,128,128]{3,2,1,0:T(8,128)} %prior_ref.3, f32[8,1]{1,0:T(8,128)} %pad.4.owners_ref), custom_call_target="tpu_custom_call" | custom-call | tf_op jit(solution)/shard_map/span_states/pallas_call | solution.py:75
  10.9 7.0 %all-to-all-start = ((f32[16,25,8,128]{3,2,1,0:T(8,128)}), f32[16,25,8,128]{3,2,1,0:T(8,128)S(1)}, u32[]{:S(2)}, u32[]{:S(2)}) async-start(f32[16,25,8,128]{3,2,1,0:T(8,128)} %span_states.1), calls=%async_computation | async-start | bytes 3276800 | tf_op jit(solution)/shard_map/all_to_all | solution.py:264
  18.0 25.2 %all-to-all-done = f32[16,25,8,128]{3,2,1,0:T(8,128)S(1)} async-done(((f32[16,25,8,128]{3,2,1,0:T(8,128)}), f32[16,25,8,128]{3,2,1,0:T(8,128)S(1)}, u32[]{:S(2)}, u32[]{:S(2)}) %all-to-all-start) | async-done | bytes 1638432 | tf_op jit(solution)/shard_map/all_to_all | solution.py:264
  43.3 0.0 copy-start.1
  43.3 1.0 constant_dynamic-slice_fusion.3
  44.3 0.3 copy-done.1
  44.6 3.1 %collective-permute-start.4 = (f32[2,25,8,128]{3,2,1,0:T(8,128)S(1)}, f32[2,25,8,128]{3,2,1,0:T(8,128)S(1)}, u32[]{:S(2)}, u32[]{:S(2)}) collective-permute-start(f32[2,25,8,128]{3,2,1,0:T(8,128)S(1)} %get-tuple-element.5), channel_id=1, source_target_pairs={{0,32},{32,64},{64,96},{96,128},{128,160},{160,192},{192,224},{224... | collective-permute-start | bytes 614408 | tf_op jit(solution)/shard_map/ppermute | solution.py:254
  47.7 0.0 collective-permute-start.5
  47.7 2.5 %collective-permute-start.6 = (f32[2,25,8,128]{3,2,1,0:T(8,128)S(1)}, f32[2,25,8,128]{3,2,1,0:T(8,128)S(1)}, u32[]{:S(2)}, u32[]{:S(2)}) collective-permute-start(f32[2,25,8,128]{3,2,1,0:T(8,128)S(1)} %get-tuple-element.3), channel_id=1, source_target_pairs={{0,64},{32,96},{64,128},{96,160},{128,192},{160,224},{192,0},{224,... | collective-permute-start | bytes 614408 | tf_op jit(solution)/shard_map/ppermute | solution.py:254
  50.2 6.1 %collective-permute-done.4.refs_1_ = f32[2,25,8,128]{3,2,1,0:T(8,128)S(1)} collective-permute-done((f32[2,25,8,128]{3,2,1,0:T(8,128)S(1)}, f32[2,25,8,128]{3,2,1,0:T(8,128)S(1)}, u32[]{:S(2)}, u32[]{:S(2)}) %collective-permute-start.4) | collective-permute-done | bytes 204832 | tf_op jit(solution)/shard_map/ppermute | solution.py:254
  56.4 0.0 copy-start.2
  56.4 0.0 collective-permute-done.5.refs_2_
  56.4 0.0 copy-start.3
  56.4 2.7 %collective-permute-done.6.refs_3_ = f32[2,25,8,128]{3,2,1,0:T(8,128)S(1)} collective-permute-done((f32[2,25,8,128]{3,2,1,0:T(8,128)S(1)}, f32[2,25,8,128]{3,2,1,0:T(8,128)S(1)}, u32[]{:S(2)}, u32[]{:S(2)}) %collective-permute-start.6) | collective-permute-done | bytes 204832 | tf_op jit(solution)/shard_map/ppermute | solution.py:254
  59.1 0.0 copy-start.4
  59.1 0.0 copy-done.2
  59.1 0.0 copy-done.3
  59.1 0.7 copy-done.4
  59.8 2.8 %address.3 = f32[16,4,2,4,8,128]{5,4,3,2,1,0:T(8,128)} custom-call(f32[2,25,8,128]{3,2,1,0:T(8,128)} %get-tuple-element.2.refs_0_, f32[2,25,8,128]{3,2,1,0:T(8,128)} %copy-done.2, f32[2,25,8,128]{3,2,1,0:T(8,128)} %copy-done.3, f32[2,25,8,128]{3,2,1,0:T(8,128)} %copy-done.4), custom_call_target="tpu_custom_call" | custom-call | tf_op jit(solution)/shard_map/address/pallas_call | solution.py:178
  62.6 4.9 %all-to-all-start.2 = ((f32[16,4,2,4,8,128]{5,4,3,2,1,0:T(8,128)}), f32[16,4,2,4,8,128]{5,4,3,2,1,0:T(8,128)S(1)}, u32[]{:S(2)}, u32[]{:S(2)}) async-start(f32[16,4,2,4,8,128]{5,4,3,2,1,0:T(8,128)} %address.3), calls=%async_computation.2 | async-start | bytes 4194304 | tf_op jit(solution)/shard_map/all_to_all | solution.py:270
  67.4 2.7 %collective-permute-start = (f32[2,25,8,128]{3,2,1,0:T(8,128)}, f32[2,25,8,128]{3,2,1,0:T(8,128)S(1)}, u32[]{:S(2)}, u32[]{:S(2)}) collective-permute-start(f32[2,25,8,128]{3,2,1,0:T(8,128)} %get-tuple-element.9), channel_id=1, source_target_pairs={{0,192},{32,224},{64,0},{96,32},{128,64},{160,96},{192,128},{224,1... | collective-permute-start | bytes 614408 | tf_op jit(solution)/shard_map/ppermute | solution.py:254
  70.2 2.7 %collective-permute-start.1 = (f32[2,25,8,128]{3,2,1,0:T(8,128)S(1)}, f32[2,25,8,128]{3,2,1,0:T(8,128)S(1)}, u32[]{:S(2)}, u32[]{:S(2)}) collective-permute-start(f32[2,25,8,128]{3,2,1,0:T(8,128)S(1)} %get-tuple-element.8), channel_id=1, source_target_pairs={{0,96},{32,128},{64,160},{96,192},{128,224},{160,0},{192,32},{224,... | collective-permute-start | bytes 614408 | tf_op jit(solution)/shard_map/ppermute | solution.py:254
  72.8 1.2 collective-permute-start.2
  74.0 4.3 %collective-permute-start.3 = (f32[2,25,8,128]{3,2,1,0:T(8,128)S(1)}, f32[2,25,8,128]{3,2,1,0:T(8,128)S(1)}, u32[]{:S(2)}, u32[]{:S(2)}) collective-permute-start(f32[2,25,8,128]{3,2,1,0:T(8,128)S(1)} %get-tuple-element.6), channel_id=1, source_target_pairs={{0,128},{32,160},{64,192},{96,224},{128,0},{160,32},{192,64},{224,... | collective-permute-start | bytes 614408 | tf_op jit(solution)/shard_map/ppermute | solution.py:254
  78.2 8.7 %collective-permute-done.refs_0_ = f32[2,25,8,128]{3,2,1,0:T(8,128)S(1)} collective-permute-done((f32[2,25,8,128]{3,2,1,0:T(8,128)}, f32[2,25,8,128]{3,2,1,0:T(8,128)S(1)}, u32[]{:S(2)}, u32[]{:S(2)}) %collective-permute-start) | collective-permute-done | bytes 204832 | tf_op jit(solution)/shard_map/ppermute | solution.py:254
  87.0 0.0 copy-start.5
  87.0 5.1 %collective-permute-done.1.refs_1_ = f32[2,25,8,128]{3,2,1,0:T(8,128)S(1)} collective-permute-done((f32[2,25,8,128]{3,2,1,0:T(8,128)S(1)}, f32[2,25,8,128]{3,2,1,0:T(8,128)S(1)}, u32[]{:S(2)}, u32[]{:S(2)}) %collective-permute-start.1) | collective-permute-done | bytes 204832 | tf_op jit(solution)/shard_map/ppermute | solution.py:254
  92.1 0.0 copy-start.6
  92.1 10.5 %collective-permute-done.2.refs_2_ = f32[2,25,8,128]{3,2,1,0:T(8,128)S(1)} collective-permute-done((f32[2,25,8,128]{3,2,1,0:T(8,128)S(1)}, f32[2,25,8,128]{3,2,1,0:T(8,128)S(1)}, u32[]{:S(2)}, u32[]{:S(2)}) %collective-permute-start.2) | collective-permute-done | bytes 204832 | tf_op jit(solution)/shard_map/ppermute | solution.py:254
  102.6 0.0 copy-start.7
  102.6 0.0 collective-permute-done.3.refs_3_
  102.6 0.0 copy-done.5
  102.6 0.0 copy-done.6
  102.6 0.7 copy-done.7
  103.3 0.7 copy-done.8
  104.0 2.8 %address.2 = f32[16,4,2,4,8,128]{5,4,3,2,1,0:T(8,128)} custom-call(f32[2,25,8,128]{3,2,1,0:T(8,128)} %copy-done.5, f32[2,25,8,128]{3,2,1,0:T(8,128)} %copy-done.6, f32[2,25,8,128]{3,2,1,0:T(8,128)} %copy-done.7, f32[2,25,8,128]{3,2,1,0:T(8,128)} %copy-done.8), custom_call_target="tpu_custom_call" | custom-call | tf_op jit(solution)/shard_map/address/pallas_call | solution.py:178
  106.8 0.0 all-to-all-done.2.got_ref
  106.8 0.0 copy-start
  106.8 1.3 copy-done
  108.2 7.0 %all-to-all-start.1 = ((f32[16,4,2,4,8,128]{5,4,3,2,1,0:T(8,128)}), f32[16,4,2,4,8,128]{5,4,3,2,1,0:T(8,128)}, u32[]{:S(2)}, u32[]{:S(2)}) async-start(f32[16,4,2,4,8,128]{5,4,3,2,1,0:T(8,128)} %address.2), calls=%async_computation.1 | async-start | bytes 4194304 | tf_op jit(solution)/shard_map/all_to_all | solution.py:270
  115.1 0.0 copy-start.10
  115.1 0.0 copy-start.9
  115.2 10.0 %span_output.1 = bf16[6,256,512]{2,1,0:T(8,128)(2,1)} custom-call(s32[6]{0:T(128)} %lengths_ref.3, bf16[6,256,512]{2,1,0:T(8,128)(2,1)} %q_ref.1, bf16[6,256,512]{2,1,0:T(8,128)(2,1)} %k_ref.3, bf16[6,256,512]{2,1,0:T(8,128)(2,1)} %v_ref.3, f32[6,4,256]{2,1,0:T(4,128)} %bitcast.10, f32[6,4,128,128]{3,2,1,0:T(8,128)} %prior_ref.3), custom_call_target="tpu_custom_call" | custom-call | flops 1409286144 | bytes 7864320 | tf_op jit(solution)/shard_map/span_output/pallas_call | solution.py:133
  125.2 0.0 copy-done.10
  125.2 0.6 compare_select_fusion.groups_ref
  125.7 0.0 copy-done.9
  125.7 0.6 compare_select_fusion.2.groups_ref
  126.3 0.8 dynamic-slice_reduce_fusion
  127.1 0.8 slice_reduce_fusion.2
  127.9 0.8 slice_reduce_fusion.1
  128.7 0.8 slice_reduce_fusion
  129.5 0.1 fusion.2
  129.6 0.5 convert_element_type.21.present_ref
  130.2 0.8 slice_reduce_fusion.6
  131.0 0.8 slice_reduce_fusion.5
  131.7 0.8 slice_reduce_fusion.4
  132.5 0.8 slice_reduce_fusion.3
  133.3 0.1 fusion.3
  133.5 0.5 convert_element_type.19.present_ref
  134.0 3.1 %place.2.refs_0_ = f32[8,8,128,128]{3,2,1,0:T(8,128)} custom-call(s32[4]{0:T(128)} %compare_select_fusion.groups_ref, s32[4]{0:T(128)} %convert_element_type.21.present_ref, f32[16,4,2,4,8,128]{5,4,3,2,1,0:T(8,128)} %copy-done), custom_call_target="tpu_custom_call" | custom-call | tf_op jit(solution)/shard_map/place/pallas_call | solution.py:231
  137.1 5.6 %all-to-all-done.1.got_ref = f32[16,4,2,4,8,128]{5,4,3,2,1,0:T(8,128)} async-done(((f32[16,4,2,4,8,128]{5,4,3,2,1,0:T(8,128)}), f32[16,4,2,4,8,128]{5,4,3,2,1,0:T(8,128)}, u32[]{:S(2)}, u32[]{:S(2)}) %all-to-all-start.1) | async-done | bytes 2097184 | tf_op jit(solution)/shard_map/all_to_all | solution.py:270
  142.7 3.1 %place.3 = f32[8,8,128,128]{3,2,1,0:T(8,128)} custom-call(s32[4]{0:T(128)} %compare_select_fusion.2.groups_ref, s32[4]{0:T(128)} %convert_element_type.19.present_ref, f32[16,4,2,4,8,128]{5,4,3,2,1,0:T(8,128)} %all-to-all-done.1.got_ref, f32[8,8,128,128]{3,2,1,0:T(8,128)} %place.2.refs_0_), custom_call_target="tpu_custom_call", output_to_operand_aliasing={{}: (3, {})} | custom-call | tf_op jit(solution)/shard_map/place/pallas_call | solution.py:231
  (2 shorter events, 0.0 us)
Async XLA Ops:
  10.9 32.3 %all-to-all-start = ((f32[16,25,8,128]{3,2,1,0:T(8,128)}), f32[16,25,8,128]{3,2,1,0:T(8,128)S(1)}, u32[]{:S(2)}, u32[]{:S(2)}) async-start(f32[16,25,8,128]{3,2,1,0:T(8,128)} %span_states.1), calls=%async_computation | async-start | bytes 3276800 | tf_op jit(solution)/shard_map/all_to_all | solution.py:264
  43.3 1.3 copy-start.1
  44.6 11.7 %collective-permute-start.4 = (f32[2,25,8,128]{3,2,1,0:T(8,128)S(1)}, f32[2,25,8,128]{3,2,1,0:T(8,128)S(1)}, u32[]{:S(2)}, u32[]{:S(2)}) collective-permute-start(f32[2,25,8,128]{3,2,1,0:T(8,128)S(1)} %get-tuple-element.5), channel_id=1, source_target_pairs={{0,32},{32,64},{64,96},{96,128},{128,160},{160,192},{192,224},{224... | collective-permute-start | bytes 614408 | tf_op jit(solution)/shard_map/ppermute | solution.py:254
  47.7 8.6 %collective-permute-start.5 = (f32[2,25,8,128]{3,2,1,0:T(8,128)S(1)}, f32[2,25,8,128]{3,2,1,0:T(8,128)S(1)}, u32[]{:S(2)}, u32[]{:S(2)}) collective-permute-start(f32[2,25,8,128]{3,2,1,0:T(8,128)S(1)} %get-tuple-element.4), channel_id=1, source_target_pairs={{0,224},{32,0},{64,32},{96,64},{128,96},{160,128},{192,160},{224,1... | collective-permute-start | bytes 614408 | tf_op jit(solution)/shard_map/ppermute | solution.py:254
  47.7 11.3 %collective-permute-start.6 = (f32[2,25,8,128]{3,2,1,0:T(8,128)S(1)}, f32[2,25,8,128]{3,2,1,0:T(8,128)S(1)}, u32[]{:S(2)}, u32[]{:S(2)}) collective-permute-start(f32[2,25,8,128]{3,2,1,0:T(8,128)S(1)} %get-tuple-element.3), channel_id=1, source_target_pairs={{0,64},{32,96},{64,128},{96,160},{128,192},{160,224},{192,0},{224,... | collective-permute-start | bytes 614408 | tf_op jit(solution)/shard_map/ppermute | solution.py:254
  56.4 2.7 %copy-start.2 = (f32[2,25,8,128]{3,2,1,0:T(8,128)}, f32[2,25,8,128]{3,2,1,0:T(8,128)S(1)}, u32[]{:S(2)}) copy-start(f32[2,25,8,128]{3,2,1,0:T(8,128)S(1)} %collective-permute-done.4.refs_1_) | copy-start | bytes 614404
  56.4 2.7 %copy-start.3 = (f32[2,25,8,128]{3,2,1,0:T(8,128)}, f32[2,25,8,128]{3,2,1,0:T(8,128)S(1)}, u32[]{:S(2)}) copy-start(f32[2,25,8,128]{3,2,1,0:T(8,128)S(1)} %collective-permute-done.5.refs_2_) | copy-start | bytes 614404
  59.1 0.7 copy-start.4
  62.6 44.2 %all-to-all-start.2 = ((f32[16,4,2,4,8,128]{5,4,3,2,1,0:T(8,128)}), f32[16,4,2,4,8,128]{5,4,3,2,1,0:T(8,128)S(1)}, u32[]{:S(2)}, u32[]{:S(2)}) async-start(f32[16,4,2,4,8,128]{5,4,3,2,1,0:T(8,128)} %address.3), calls=%async_computation.2 | async-start | bytes 4194304 | tf_op jit(solution)/shard_map/all_to_all | solution.py:270
  67.4 19.6 %collective-permute-start = (f32[2,25,8,128]{3,2,1,0:T(8,128)}, f32[2,25,8,128]{3,2,1,0:T(8,128)S(1)}, u32[]{:S(2)}, u32[]{:S(2)}) collective-permute-start(f32[2,25,8,128]{3,2,1,0:T(8,128)} %get-tuple-element.9), channel_id=1, source_target_pairs={{0,192},{32,224},{64,0},{96,32},{128,64},{160,96},{192,128},{224,1... | collective-permute-start | bytes 614408 | tf_op jit(solution)/shard_map/ppermute | solution.py:254
  70.2 21.9 %collective-permute-start.1 = (f32[2,25,8,128]{3,2,1,0:T(8,128)S(1)}, f32[2,25,8,128]{3,2,1,0:T(8,128)S(1)}, u32[]{:S(2)}, u32[]{:S(2)}) collective-permute-start(f32[2,25,8,128]{3,2,1,0:T(8,128)S(1)} %get-tuple-element.8), channel_id=1, source_target_pairs={{0,96},{32,128},{64,160},{96,192},{128,224},{160,0},{192,32},{224,... | collective-permute-start | bytes 614408 | tf_op jit(solution)/shard_map/ppermute | solution.py:254
  72.8 29.8 %collective-permute-start.2 = (f32[2,25,8,128]{3,2,1,0:T(8,128)S(1)}, f32[2,25,8,128]{3,2,1,0:T(8,128)S(1)}, u32[]{:S(2)}, u32[]{:S(2)}) collective-permute-start(f32[2,25,8,128]{3,2,1,0:T(8,128)S(1)} %get-tuple-element.7), channel_id=1, source_target_pairs={{0,160},{32,192},{64,224},{96,0},{128,32},{160,64},{192,96},{224,1... | collective-permute-start | bytes 614408 | tf_op jit(solution)/shard_map/ppermute | solution.py:254
  74.0 28.7 %collective-permute-start.3 = (f32[2,25,8,128]{3,2,1,0:T(8,128)S(1)}, f32[2,25,8,128]{3,2,1,0:T(8,128)S(1)}, u32[]{:S(2)}, u32[]{:S(2)}) collective-permute-start(f32[2,25,8,128]{3,2,1,0:T(8,128)S(1)} %get-tuple-element.6), channel_id=1, source_target_pairs={{0,128},{32,160},{64,192},{96,224},{128,0},{160,32},{192,64},{224,... | collective-permute-start | bytes 614408 | tf_op jit(solution)/shard_map/ppermute | solution.py:254
  87.0 15.7 %copy-start.5 = (f32[2,25,8,128]{3,2,1,0:T(8,128)}, f32[2,25,8,128]{3,2,1,0:T(8,128)S(1)}, u32[]{:S(2)}) copy-start(f32[2,25,8,128]{3,2,1,0:T(8,128)S(1)} %collective-permute-done.refs_0_) | copy-start | bytes 614404
  92.1 10.6 %copy-start.6 = (f32[2,25,8,128]{3,2,1,0:T(8,128)}, f32[2,25,8,128]{3,2,1,0:T(8,128)S(1)}, u32[]{:S(2)}) copy-start(f32[2,25,8,128]{3,2,1,0:T(8,128)S(1)} %collective-permute-done.1.refs_1_) | copy-start | bytes 614404
  102.6 0.7 copy-start.7
  103.3 0.7 copy-start.8
  106.8 1.3 copy-start
  108.2 34.5 %all-to-all-start.1 = ((f32[16,4,2,4,8,128]{5,4,3,2,1,0:T(8,128)}), f32[16,4,2,4,8,128]{5,4,3,2,1,0:T(8,128)}, u32[]{:S(2)}, u32[]{:S(2)}) async-start(f32[16,4,2,4,8,128]{5,4,3,2,1,0:T(8,128)} %address.2), calls=%async_computation.1 | async-start | bytes 4194304 | tf_op jit(solution)/shard_map/all_to_all | solution.py:270
  115.1 10.0 %copy-start.10 = (s32[4]{0:T(128)S(1)}, s32[4]{0:T(128)}, u32[]{:S(2)}) copy-start(s32[4]{0:T(128)} %constant.73) | copy-start | bytes 52
  115.1 10.6 %copy-start.9 = (s32[4]{0:T(128)S(1)}, s32[4]{0:T(128)}, u32[]{:S(2)}) copy-start(s32[4]{0:T(128)} %constant.72) | copy-start | bytes 52

commit v3 on v2

--- a/solution.py
+++ b/solution.py
@@ -10,7 +10,11 @@
 HD = 128
 ROWS = 8
 VMEM = 56 << 20
-SHIFTS = ((0, 1, 7, 2), (6, 3, 5, 4))
+PARTS = 2
+STEPS = 2
+ORDER = (0, 1, 7, 2, 6, 3, 5, 4)
+LATE = 5
+FIRST = 0
 
 
 def head_of(h):
@@ -39,57 +43,107 @@
     )
 
 
-def state_kernel(lengths_ref, k_ref, v_ref, ld_ref, prior_ref, owners_ref, out_ref):
-    r = pl.program_id(0)
-    length = lengths_ref[r]
-    heads, tokens = ld_ref.shape[1:]
-    live_row = lax.broadcasted_iota(jnp.int32, (heads, tokens), 1) < length
-    total = column_sums(jnp.where(live_row, ld_ref[0], 0.0))
-    last = total[tokens - 1:tokens, :]
-    live_col = lax.broadcasted_iota(jnp.int32, (tokens, heads), 0) < length
-    keep = jnp.where(live_col, jnp.exp(last - total), 0.0)
+def split_three(x):
+    high = x.astype(jnp.bfloat16).astype(jnp.float32)
+    rest = x - high
+    mid = rest.astype(jnp.bfloat16).astype(jnp.float32)
+    return high, mid, rest - mid
+
+
+def final_states(length, p, k_ref, v_ref, rate, prior_ref, upper):
+    heads, tokens = rate.shape
+    live = lax.broadcasted_iota(jnp.int32, (heads, tokens), 1) < length
+    terms = jnp.concatenate(split_three(jnp.where(live, rate, 0.0)), axis=0).astype(jnp.bfloat16)
+    sums = jnp.dot(terms, upper, preferred_element_type=jnp.float32)
+    total = sums[2 * heads:] + sums[heads:2 * heads] + sums[:heads]
+    last = total[:, tokens - 1:tokens]
+    keep = jnp.where(live, jnp.exp(last - total), 0.0)
     final = jnp.exp(last)
+    states = []
     for h in range(heads):
-        k = k_ref[0, :, head_of(h)].astype(jnp.float32)
-        decayed = (k * keep[:, h:h + 1]).astype(jnp.bfloat16)
-        fresh = lax.dot_general(
-            decayed, v_ref[0, :, head_of(h)], (((0,), (0,)), ((), ())),
-            preferred_element_type=jnp.float32,
-        )
-        state = final[:, h:h + 1] * prior_ref[0, h] + fresh
-        out_ref[:, r * heads + h] = state.reshape(HD // ROWS, ROWS, HD)
-
-    @pl.when(r == 0)
+        k = k_ref[p, :, head_of(h)].astype(jnp.float32).T
+        decayed = (k * keep[h:h + 1, :]).astype(jnp.bfloat16)
+        fresh = jnp.dot(decayed, v_ref[p, :, head_of(h)], preferred_element_type=jnp.float32)
+        states.append(final[h:h + 1, :] * prior_ref[p, h] + fresh)
+    return states
+
+
+def fill_upper(upper_ref):
+    row = lax.broadcasted_iota(jnp.int32, upper_ref.shape, 0)
+    col = lax.broadcasted_iota(jnp.int32, upper_ref.shape, 1)
+    upper_ref[...] = jnp.where(row <= col, 1.0, 0.0).astype(jnp.bfloat16)
+
+
+def mixing_kernel(first, lengths_ref, owners_ref, k_ref, v_ref, ld_ref, prior_ref, out_ref, upper_ref):
+    step = pl.program_id(0)
+    each, heads = prior_ref.shape[:2]
+
+    @pl.when(step == 0)
     def _():
-        named = jnp.broadcast_to(owners_ref[...], out_ref.shape[2:])
+        fill_upper(upper_ref)
+        row = lax.broadcasted_iota(jnp.int32, out_ref.shape[2:], 0)
+        named = jnp.zeros(out_ref.shape[2:], jnp.int32)
+        for i in range(owners_ref.shape[0]):
+            named = jnp.where(row == i, owners_ref[i], named)
         for j in range(out_ref.shape[0]):
-            out_ref[j, out_ref.shape[1] - 1] = named
-
-
-def span_states(lengths, keys, values, ld, prior, owners):
+            out_ref[j, out_ref.shape[1] - 1] = named.astype(jnp.float32)
+
+    for p in range(each):
+        r = step * each + p
+        rate = ld_ref[p, first:first + heads]
+        states = final_states(lengths_ref[r], p, k_ref, v_ref, rate, prior_ref, upper_ref[...])
+        for h in range(heads):
+            out_ref[:, r * heads + h] = states[h].reshape(HD // ROWS, ROWS, HD)
+
+
+def owner_kernel(first, lengths_ref, owners_ref, k_ref, v_ref, ld_ref, prior_ref, out_ref, upper_ref):
+    step = pl.program_id(0)
+    each, heads = prior_ref.shape[:2]
+
+    @pl.when(step == 0)
+    def _():
+        fill_upper(upper_ref)
+
+    for p in range(each):
+        r = step * each + p
+        rate = ld_ref[p, first:first + heads]
+        states = final_states(lengths_ref[r], p, k_ref, v_ref, rate, prior_ref, upper_ref[...])
+        for h in range(heads):
+            out_ref[owners_ref[r], h] = states[h]
+
+
+def span_states(mixing, first, per, lengths, owned, keys, values, ld, prior, count):
     prompts, tokens, width = keys.shape
     heads = ld.shape[1]
-    pieces = HD // ROWS
-    named = jnp.pad(owners.astype(jnp.float32), ((0, ROWS - prompts), (0, 0)))
-    shape = (pieces, prompts * heads + 1, ROWS, HD)
+    each = prompts // STEPS
+    block = first // per
+    if mixing:
+        shape = (HD // ROWS, prompts * per + 1, ROWS, HD)
+    else:
+        shape = (count, per, HD, HD)
     return pl.pallas_call(
-        state_kernel,
+        functools.partial(mixing_kernel if mixing else owner_kernel, first),
         grid_spec=pltpu.PrefetchScalarGridSpec(
-            num_scalar_prefetch=1,
-            grid=(prompts,),
+            num_scalar_prefetch=2,
+            grid=(STEPS,),
             in_specs=[
-                pl.BlockSpec((1, tokens, width), lambda r, s: (r, 0, 0)),
-                pl.BlockSpec((1, tokens, width), lambda r, s: (r, 0, 0)),
-                pl.BlockSpec((1, heads, tokens), lambda r, s: (r, 0, 0)),
-                pl.BlockSpec((1, heads, HD, HD), lambda r, s: (r, 0, 0, 0)),
-                pl.BlockSpec((ROWS, 1), lambda r, s: (0, 0)),
+                pl.BlockSpec((each, tokens, per * HD), lambda r, s, o: (r, 0, block)),
+                pl.BlockSpec((each, tokens, per * HD), lambda r, s, o: (r, 0, block)),
+                pl.BlockSpec((each, heads, tokens), lambda r, s, o: (r, 0, 0)),
+                pl.BlockSpec((each, per, HD, HD), lambda r, s, o: (r, block, 0, 0)),
             ],
-            out_specs=pl.BlockSpec(shape, lambda r, s: (0, 0, 0, 0)),
+            out_specs=pl.BlockSpec(shape, lambda r, s, o: (0, 0, 0, 0)),
+            scratch_shapes=[pltpu.VMEM((tokens, tokens), jnp.bfloat16)],
         ),
         out_shape=jax.ShapeDtypeStruct(shape, jnp.float32),
         compiler_params=pltpu.CompilerParams(vmem_limit_bytes=VMEM),
+        cost_estimate=pl.CostEstimate(
+            flops=2 * prompts * per * tokens * HD * HD,
+            bytes_accessed=4 * prompts * tokens * per * HD + 8 * prompts * per * HD * HD,
+            transcendentals=prompts * per * tokens,
+        ),
         name="span_states",
-    )(lengths, keys, values, ld, prior, named)
+    )(lengths, owned, keys, values, ld, prior)
 
 
 def output_kernel(lengths_ref, q_ref, k_ref, v_ref, ld_ref, prior_ref, out_ref):
@@ -153,33 +207,46 @@
     )(lengths, queries, keys, values, ld, prior)
 
 
-def address_kernel(slots, *refs):
+def address_kernel(slots, n_pre, where_ref, *refs):
     held = refs[:slots]
-    out_ref, names, name_sems, sems = refs[slots:]
+    out_ref, groups_ref, present_ref, names, name_sems, sems = refs[slots:]
     per = out_ref.shape[3]
     rows = held[0].shape[1] - 1
-    for j in range(slots):
-        pltpu.make_async_copy(held[j].at[0, rows], names.at[j], name_sems.at[j]).start()
-    for j in range(slots):
-        pltpu.make_async_copy(held[j].at[0, rows], names.at[j], name_sems.at[j]).wait()
+
+    def fetch(j):
+        return pltpu.make_async_copy(held[j].at[0, rows], names.at[j], name_sems.at[j])
+
+    for j in range(slots):
+        fetch(j).start()
+    for j in range(slots):
+        fetch(j).wait()
+        groups_ref[j] = lax.rem(where_ref[0] + n_pre - ORDER[j], n_pre)
+        present = jnp.int32(0)
         for r in range(rows // per):
             owner = names[j, r, 0].astype(jnp.int32)
+            present = jnp.where(owner == where_ref[1], 1, present)
             pltpu.make_async_copy(
                 held[j].at[:, pl.ds(r * per, per)], out_ref.at[owner, j], sems.at[j]
             ).start()
+        present_ref[j] = present
     for j in range(slots):
         sent = held[j].at[:, pl.ds(0, rows)]
         pltpu.make_async_copy(sent, sent, sems.at[j]).wait()
 
 
-def address(held, count, heads):
+def address(where, held, count, per):
     slots = len(held)
     halves = held[0].shape[0]
+    smem = pl.BlockSpec(memory_space=pltpu.SMEM)
     return pl.pallas_call(
-        functools.partial(address_kernel, slots),
-        in_specs=[pl.BlockSpec(memory_space=pltpu.VMEM) for _ in held],
-        out_specs=pl.BlockSpec(memory_space=pl.ANY),
-        out_shape=jax.ShapeDtypeStruct((count, slots, halves, heads, ROWS, HD), jnp.float32),
+        functools.partial(address_kernel, slots, len(ORDER)),
+        in_specs=[smem] + [pl.BlockSpec(memory_space=pltpu.VMEM) for _ in held],
+        out_specs=[pl.BlockSpec(memory_space=pl.ANY), smem, smem],
+        out_shape=[
+            jax.ShapeDtypeStruct((count, slots, halves, per, ROWS, HD), jnp.float32),
+            jax.ShapeDtypeStruct((slots,), jnp.int32),
+            jax.ShapeDtypeStruct((slots,), jnp.int32),
+        ],
         scratch_shapes=[
             pltpu.SMEM((slots, ROWS, HD), jnp.float32),
             pltpu.SemaphoreType.DMA((slots,)),
@@ -187,18 +254,17 @@
         ],
         compiler_params=pltpu.CompilerParams(vmem_limit_bytes=VMEM),
         name="address",
-    )(*held)
-
-
-def place_kernel(groups_ref, present_ref, got_ref, *refs):
-    out_ref, got, placed, in_sems, out_sems = refs[-5:]
+    )(where, *held)
+
+
+def place_rows_kernel(groups_ref, present_ref, got_ref, out_ref, got, placed, in_sems, out_sems):
     pieces, slots, halves, per = got_ref.shape[:4]
 
     def fetch(j):
         return pltpu.make_async_copy(got_ref.at[:, j], got.at[j], in_sems.at[j])
 
     def store(j):
-        return pltpu.make_async_copy(placed.at[j], out_ref.at[groups_ref[j]], out_sems.at[j])
+        return pltpu.make_async_copy(placed.at[j], out_ref.at[groups_ref[j], :, 0], out_sems.at[j])
 
     for j in range(slots):
         @pl.when(present_ref[j] > 0)
@@ -215,34 +281,69 @@
             fetch(j).wait()
             for b in range(halves):
                 for e in range(per):
-                    placed[j, b * per + e] = got[j, :, b, e].reshape(pieces * ROWS, HD)
+                    placed[j, b, e] = got[j, :, b, e].reshape(pieces * ROWS, HD)
 
         store(j).start()
     for j in range(slots):
         store(j).wait()
 
 
-def place(groups, present, got, n_groups, out=None):
+def place_rows(groups, present, got, n_groups):
     pieces, slots, halves, per = got.shape[:4]
-    heads = halves * per
     smem = pl.BlockSpec(memory_space=pltpu.SMEM)
     hbm = pl.BlockSpec(memory_space=pl.ANY)
-    given = [groups, present, got] + ([] if out is None else [out])
     return pl.pallas_call(
-        place_kernel,
-        in_specs=[smem, smem, hbm] + ([] if out is None else [hbm]),
+        place_rows_kernel,
+        in_specs=[smem, smem, hbm],
         out_specs=hbm,
-        out_shape=jax.ShapeDtypeStruct((n_groups, heads, HD, HD), jnp.float32),
-        input_output_aliases={} if out is None else {3: 0},
+        out_shape=jax.ShapeDtypeStruct((n_groups, halves, PARTS, per, HD, HD), jnp.float32),
         scratch_shapes=[
             pltpu.VMEM((slots, pieces, halves, per, ROWS, HD), jnp.float32),
-            pltpu.VMEM((slots, heads, HD, HD), jnp.float32),
+            pltpu.VMEM((slots, halves, per, HD, HD), jnp.float32),
             pltpu.SemaphoreType.DMA((slots,)),
             pltpu.SemaphoreType.DMA((slots,)),
         ],
         compiler_params=pltpu.CompilerParams(vmem_limit_bytes=VMEM),
-        name="place",
-    )(*given)
+        name="place_rows",
+    )(groups, present, got)
+
+
+def place_blocks_kernel(first, slots, groups_ref, present_ref, *refs):
+    got = refs[:slots]
+    out_ref, empty, sems = refs[slots + 1:]
+    empty[...] = jnp.zeros(empty.shape, jnp.float32)
+    for j in range(slots):
+        target = out_ref.at[groups_ref[first + j], :, 1]
+
+        @pl.when(present_ref[first + j] > 0)
+        def _():
+            pltpu.make_async_copy(got[j], target, sems.at[j]).start()
+
+        @pl.when(present_ref[first + j] == 0)
+        def _():
+            pltpu.make_async_copy(empty, target, sems.at[j]).start()
+
+    for j in range(slots):
+        pltpu.make_async_copy(empty, empty, sems.at[j]).wait()
+
+
+def place_blocks(first, groups, present, got, out):
+    slots = len(got)
+    smem = pl.BlockSpec(memory_space=pltpu.SMEM)
+    hbm = pl.BlockSpec(memory_space=pl.ANY)
+    return pl.pallas_call(
+        functools.partial(place_blocks_kernel, first, slots),
+        in_specs=[smem, smem] + [pl.BlockSpec(memory_space=pltpu.VMEM)] * slots + [hbm],
+        out_specs=hbm,
+        out_shape=jax.ShapeDtypeStruct(out.shape, jnp.float32),
+        input_output_aliases={2 + slots: 0},
+        scratch_shapes=[
+            pltpu.VMEM(got[0].shape, jnp.float32),
+            pltpu.SemaphoreType.DMA((slots,)),
+        ],
+        compiler_params=pltpu.CompilerParams(vmem_limit_bytes=VMEM),
+        name="place_blocks",
+    )(groups, present, *got, out)
 
 
 def shifted(mixed, shift, n_pre):
@@ -254,26 +355,32 @@
     return lax.ppermute(part, "pre", [(i, (i + shift) % n_pre) for i in range(n_pre)])
 
 
+def over_dec(x):
+    return lax.all_to_all(x, "dec", split_axis=0, concat_axis=0, tiled=True)
+
+
 def shards(queries, keys, values, log_decay, prior_state, lengths, owners):
     n_pre = lax.axis_size("pre")
     n_dec = lax.axis_size("dec")
-    prompts, heads = prior_state.shape[:2]
-    me_pre, me_dec = lax.axis_index("pre"), lax.axis_index("dec")
+    heads = prior_state.shape[1]
     ld = jnp.swapaxes(log_decay, 1, 2)
-    states = span_states(lengths, keys, values, ld, prior_state, owners)
-    mixed = lax.all_to_all(states, "dec", split_axis=0, concat_axis=0, tiled=True)
-    held = {m: shifted(mixed, m, n_pre) for batch in SHIFTS for m in batch}
-    decode_state = None
-    for batch in SHIFTS:
-        blocks = [held[m] for m in batch]
-        sent = address(blocks, n_dec, heads)
-        got = lax.all_to_all(sent, "dec", split_axis=0, concat_axis=0, tiled=True)
-        named = jnp.stack([x[0, -1, :prompts, 0] for x in blocks]).astype(jnp.int32)
-        present = jnp.any(named == me_dec, axis=1).astype(jnp.int32)
-        groups = lax.rem(me_pre + n_pre - jnp.array(batch, jnp.int32), n_pre)
-        decode_state = place(groups, present, got, n_pre, decode_state)
+    spans = (lengths, owners[:, 0], keys, values, ld, prior_state, n_dec)
+    per = heads // PARTS
+    where = jnp.stack([lax.axis_index("pre"), lax.axis_index("dec")]).astype(jnp.int32)
+    mixed = over_dec(span_states(True, 0, per, *spans))
+    named = span_states(False, per, per, *spans)
     prefill_out = span_output(lengths, queries, keys, values, ld, prior_state)
-    return prefill_out, decode_state
+    named, mixed, prefill_out, where = lax.optimization_barrier((named, mixed, prefill_out, where))
+    owned = over_dec(named)
+    held = [shifted(mixed, m, n_pre) for m in ORDER]
+    blocks = [shifted(owned, m, n_pre) for m in ORDER]
+    held, blocks[:FIRST] = lax.optimization_barrier((held, blocks[:FIRST]))
+    sent, groups, present = address(where, held, n_dec, per)
+    got = over_dec(sent)
+    decode_state = place_rows(groups, present, got, n_pre)
+    decode_state = place_blocks(0, groups, present, blocks[:LATE], decode_state)
+    decode_state = place_blocks(LATE, groups, present, blocks[LATE:], decode_state)
+    return prefill_out, decode_state.reshape(n_pre, -1, HD, HD)
 
 
 def solution(mesh):

time: 147 us -> 128 us (0.87)
  the two profiles are of different devices: /device:TPU:96 before, /device:TPU:2 now
where the time goes in v3:
time: 128 us; the launch traced here: 127 us
  starting transfers between devices  55.8 us (44%)
  waiting for transfers between devices  35.4 us (28%)
  Pallas kernels  30.8 us (24%)
  local copies, waits for them, and re-layouts  3.75 us (3%)
    ppermute x14, starting transfers between devices, shifted(): lax.ppermute(part, 'pre', [(i, (i + shift) % n_pre) for i in range(n_pre)])  33.8 us
    ppermute x14, waiting for transfers between devices, shifted(): lax.ppermute(part, 'pre', [(i, (i + shift) % n_pre) for i in range(n_pre)])  29.2 us
    all_to_all x3, starting transfers between devices, over_dec(): return lax.all_to_all(x, 'dec', split_axis=0, concat_axis=0, tiled=True)  21.9 us
    pallas_call x1, Pallas kernels, span_output(): pl.pallas_call(output_kernel, grid_spec=pltpu.PrefetchScalarGridSpec(num_...  9.87 us
    pallas_call x2, Pallas kernels, span_states(): pl.pallas_call(functools.partial(mixing_kernel if mixing else owner_kerne...  9.83 us
    all_to_all x3, waiting for transfers between devices, over_dec(): return lax.all_to_all(x, 'dec', split_axis=0, concat_axis=0, tiled=True)  6.18 us
    pallas_call x2, Pallas kernels, place_blocks(): pl.pallas_call(functools.partial(place_blocks_kernel, first, slots), in_s...  4.41 us
    pallas_call x1, Pallas kernels, address(): pl.pallas_call(functools.partial(address_kernel, slots, len(ORDER)), in_s...  3.6 us
  transfers between devices with their start and end apart: 17, of which 9 were waited for; matrix products, arithmetic and copies ran while one was open for 2% of the time, Pallas kernels for 19%

profile of v3, /device:TPU:2, one launch (start us, length us, event | category | flops | bytes accessed | tf_op | source)
XLA Modules:
  0.0 127.2 jit_solution(7300283483185187214)
XLA Ops:
  0.6 4.7 %span_states.3 = f32[16,13,8,128]{3,2,1,0:T(8,128)} custom-call(s32[6]{0:T(128)} %lengths_ref.5, s32[6]{0:T(128)} %bitcast.9, bf16[6,256,512]{2,1,0:T(8,128)(2,1)} %k_ref.5, bf16[6,256,512]{2,1,0:T(8,128)(2,1)} %v_ref.5, f32[6,4,256]{2,1,0:T(4,128)} %bitcast.6, f32[6,4,128,128]{3,2,1,0:T(8,128)} %prior_ref.5), custom_call_target="tpu_custom_call" | custom-call | flops 100663296 | bytes 3145728 | tf_op jit(solution)/shard_map/span_states/pallas_call | solution.py:124
  5.3 7.5 %all-to-all-start = ((f32[16,13,8,128]{3,2,1,0:T(8,128)}), f32[16,13,8,128]{3,2,1,0:T(8,128)S(1)}, u32[]{:S(2)}, u32[]{:S(2)}) async-start(f32[16,13,8,128]{3,2,1,0:T(8,128)} %span_states.3), calls=%async_computation | async-start | bytes 1703936 | tf_op jit(solution)/shard_map/all_to_all | solution.py:359
  12.8 5.1 %span_states.2 = f32[16,2,128,128]{3,2,1,0:T(8,128)} custom-call(s32[6]{0:T(128)} %lengths_ref.5, s32[6]{0:T(128)} %bitcast.10, bf16[6,256,512]{2,1,0:T(8,128)(2,1)} %k_ref.5, bf16[6,256,512]{2,1,0:T(8,128)(2,1)} %v_ref.5, f32[6,4,256]{2,1,0:T(4,128)} %bitcast.7, f32[6,4,128,128]{3,2,1,0:T(8,128)} %prior_ref.5), custom_call_target="tpu_custom_call" | custom-call | flops 100663296 | bytes 3145728 | tf_op jit(solution)/shard_map/span_states/pallas_call | solution.py:124
  17.9 0.7 pad_add_fusion.where_ref
  18.6 9.9 %span_output.1 = bf16[6,256,512]{2,1,0:T(8,128)(2,1)} custom-call(s32[6]{0:T(128)} %lengths_ref.5, bf16[6,256,512]{2,1,0:T(8,128)(2,1)} %q_ref.1, bf16[6,256,512]{2,1,0:T(8,128)(2,1)} %k_ref.5, bf16[6,256,512]{2,1,0:T(8,128)(2,1)} %v_ref.5, f32[6,4,256]{2,1,0:T(4,128)} %bitcast.8, f32[6,4,128,128]{3,2,1,0:T(8,128)} %prior_ref.5), custom_call_target="tpu_custom_call" | custom-call | flops 1409286144 | bytes 7864320 | tf_op jit(solution)/shard_map/span_output/pallas_call | solution.py:187
  28.5 0.0 all-to-all-done
  28.5 7.2 %all-to-all-start.1 = ((f32[16,2,128,128]{3,2,1,0:T(8,128)}), f32[16,2,128,128]{3,2,1,0:T(8,128)S(1)}, u32[]{:S(2)}, u32[]{:S(2)}) async-start(f32[16,2,128,128]{3,2,1,0:T(8,128)} %span_states.2), calls=%async_computation.1 | async-start | bytes 4194304 | tf_op jit(solution)/shard_map/all_to_all | solution.py:359
  35.7 0.7 constant_dynamic-slice_fusion.8
  36.4 7.2 %collective-permute-start.6 = (f32[2,13,8,128]{3,2,1,0:T(8,128)S(1)}, f32[2,13,8,128]{3,2,1,0:T(8,128)S(1)}, u32[]{:S(2)}, u32[]{:S(2)}) collective-permute-start(f32[2,13,8,128]{3,2,1,0:T(8,128)S(1)} %get-tuple-element.40), channel_id=1, source_target_pairs={{0,128},{32,160},{64,192},{96,224},{128,0},{160,32},{192,64},{224,... | collective-permute-start | bytes 319496 | tf_op jit(solution)/shard_map/ppermute | solution.py:355
  43.6 0.0 collective-permute-start.5
  43.6 3.8 %collective-permute-start.4 = (f32[2,13,8,128]{3,2,1,0:T(8,128)S(1)}, f32[2,13,8,128]{3,2,1,0:T(8,128)S(1)}, u32[]{:S(2)}, u32[]{:S(2)}) collective-permute-start(f32[2,13,8,128]{3,2,1,0:T(8,128)S(1)} %get-tuple-element.42), channel_id=1, source_target_pairs={{0,96},{32,128},{64,160},{96,192},{128,224},{160,0},{192,32},{224,... | collective-permute-start | bytes 319496 | tf_op jit(solution)/shard_map/ppermute | solution.py:355
  47.4 0.9 collective-permute-start.3
  48.3 2.1 %collective-permute-start.2 = (f32[2,13,8,128]{3,2,1,0:T(8,128)S(1)}, f32[2,13,8,128]{3,2,1,0:T(8,128)S(1)}, u32[]{:S(2)}, u32[]{:S(2)}) collective-permute-start(f32[2,13,8,128]{3,2,1,0:T(8,128)S(1)} %get-tuple-element.44), channel_id=1, source_target_pairs={{0,64},{32,96},{64,128},{96,160},{128,192},{160,224},{192,0},{224,... | collective-permute-start | bytes 319496 | tf_op jit(solution)/shard_map/ppermute | solution.py:355
  50.3 0.0 collective-permute-done.6.refs_7_
  50.3 0.0 copy-start.7
  50.3 2.7 %collective-permute-start.1 = (f32[2,13,8,128]{3,2,1,0:T(8,128)S(1)}, f32[2,13,8,128]{3,2,1,0:T(8,128)S(1)}, u32[]{:S(2)}, u32[]{:S(2)}) collective-permute-start(f32[2,13,8,128]{3,2,1,0:T(8,128)S(1)} %get-tuple-element.45), channel_id=1, source_target_pairs={{0,224},{32,0},{64,32},{96,64},{128,96},{160,128},{192,160},{224,1... | collective-permute-start | bytes 319496 | tf_op jit(solution)/shard_map/ppermute | solution.py:355
  53.1 2.2 %collective-permute-done.5.refs_6_ = f32[2,13,8,128]{3,2,1,0:T(8,128)S(1)} collective-permute-done((f32[2,13,8,128]{3,2,1,0:T(8,128)S(1)}, f32[2,13,8,128]{3,2,1,0:T(8,128)S(1)}, u32[]{:S(2)}, u32[]{:S(2)}) %collective-permute-start.5) | collective-permute-done | bytes 106528 | tf_op jit(solution)/shard_map/ppermute | solution.py:355
  55.2 4.3 %collective-permute-start = (f32[2,13,8,128]{3,2,1,0:T(8,128)S(1)}, f32[2,13,8,128]{3,2,1,0:T(8,128)S(1)}, u32[]{:S(2)}, u32[]{:S(2)}) collective-permute-start(f32[2,13,8,128]{3,2,1,0:T(8,128)S(1)} %get-tuple-element.46), channel_id=1, source_target_pairs={{0,32},{32,64},{64,96},{96,128},{128,160},{160,192},{192,224},{224... | collective-permute-start | bytes 319496 | tf_op jit(solution)/shard_map/ppermute | solution.py:355
  59.6 0.0 collective-permute-done.4.refs_5_
  59.6 0.0 copy-start.9
  59.6 0.3 collective-permute-done.3.refs_4_
  59.9 0.0 copy-start.10
  59.9 0.0 collective-permute-done.2.refs_3_
  59.9 0.0 copy-start.11
  59.9 2.3 %collective-permute-done.1.refs_2_ = f32[2,13,8,128]{3,2,1,0:T(8,128)S(1)} collective-permute-done((f32[2,13,8,128]{3,2,1,0:T(8,128)S(1)}, f32[2,13,8,128]{3,2,1,0:T(8,128)S(1)}, u32[]{:S(2)}, u32[]{:S(2)}) %collective-permute-start.1) | collective-permute-done | bytes 106528 | tf_op jit(solution)/shard_map/ppermute | solution.py:355
  62.2 0.0 copy-start.12
  62.2 0.0 collective-permute-done.refs_1_
  62.2 0.0 copy-done.7
  62.2 0.0 copy-done.8
  62.2 0.0 copy-done.9
  62.2 0.0 copy-done.10
  62.2 0.0 copy-done.11
  62.2 0.6 copy-done.12
  62.8 0.0 copy-done.13
  62.9 3.6 %address.1 = (f32[16,8,2,2,8,128]{5,4,3,2,1,0:T(8,128)}, s32[8]{0:T(128)}, s32[8]{0:T(128)}) custom-call(s32[2]{0:T(128)} %pad_add_fusion.where_ref, f32[2,13,8,128]{3,2,1,0:T(8,128)} %get-tuple-element.20.refs_0_, f32[2,13,8,128]{3,2,1,0:T(8,128)} %copy-done.13, f32[2,13,8,128]{3,2,1,0:T(8,128)} %copy-done.12, f32[2,13,8,128]{3,2,1,0:T(8,128)} %copy-done.11, ...), custom_call_target="tpu_custom_call" | custom-call | tf_op jit(solution)/shard_map/address/pallas_call | solution.py:241
  66.5 0.0 all-to-all-done.1
  66.5 7.2 %all-to-all-start.2 = ((f32[16,8,2,2,8,128]{5,4,3,2,1,0:T(8,128)}), f32[16,8,2,2,8,128]{5,4,3,2,1,0:T(8,128)}, u32[]{:S(2)}, u32[]{:S(2)}) async-start(f32[16,8,2,2,8,128]{5,4,3,2,1,0:T(8,128)} %get-tuple-element.31), calls=%async_computation.2 | async-start | bytes 4194304 | tf_op jit(solution)/shard_map/all_to_all | solution.py:359
  73.7 0.9 constant_dynamic-slice_fusion
  74.6 3.4 %collective-permute-start.13 = (f32[2,2,128,128]{3,2,1,0:T(8,128)S(1)}, f32[2,2,128,128]{3,2,1,0:T(8,128)S(1)}, u32[]{:S(2)}, u32[]{:S(2)}) collective-permute-start(f32[2,2,128,128]{3,2,1,0:T(8,128)S(1)} %get-tuple-element.32), channel_id=1, source_target_pairs={{0,192},{32,224},{64,0},{96,32},{128,64},{160,96},{192,128},{224,1... | collective-permute-start | bytes 786440 | tf_op jit(solution)/shard_map/ppermute | solution.py:355
  78.0 0.0 collective-permute-start.12
  78.0 3.1 %collective-permute-start.11 = (f32[2,2,128,128]{3,2,1,0:T(8,128)S(1)}, f32[2,2,128,128]{3,2,1,0:T(8,128)S(1)}, u32[]{:S(2)}, u32[]{:S(2)}) collective-permute-start(f32[2,2,128,128]{3,2,1,0:T(8,128)S(1)} %get-tuple-element.34), channel_id=1, source_target_pairs={{0,224},{32,0},{64,32},{96,64},{128,96},{160,128},{192,160},{224,1... | collective-permute-start | bytes 786440 | tf_op jit(solution)/shard_map/ppermute | solution.py:355
  81.1 0.0 collective-permute-start.10
  81.1 2.8 %collective-permute-start.9 = (f32[2,2,128,128]{3,2,1,0:T(8,128)S(1)}, f32[2,2,128,128]{3,2,1,0:T(8,128)S(1)}, u32[]{:S(2)}, u32[]{:S(2)}) collective-permute-start(f32[2,2,128,128]{3,2,1,0:T(8,128)S(1)} %get-tuple-element.37), channel_id=1, source_target_pairs={{0,128},{32,160},{64,192},{96,224},{128,0},{160,32},{192,64},{224,... | collective-permute-start | bytes 786440 | tf_op jit(solution)/shard_map/ppermute | solution.py:355
  84.0 5.0 %collective-permute-done.13.refs_4_ = f32[2,2,128,128]{3,2,1,0:T(8,128)S(1)} collective-permute-done((f32[2,2,128,128]{3,2,1,0:T(8,128)S(1)}, f32[2,2,128,128]{3,2,1,0:T(8,128)S(1)}, u32[]{:S(2)}, u32[]{:S(2)}) %collective-permute-start.13) | collective-permute-done | bytes 262176 | tf_op jit(solution)/shard_map/ppermute | solution.py:355
  89.0 3.0 %collective-permute-start.8 = (f32[2,2,128,128]{3,2,1,0:T(8,128)S(1)}, f32[2,2,128,128]{3,2,1,0:T(8,128)S(1)}, u32[]{:S(2)}, u32[]{:S(2)}) collective-permute-start(f32[2,2,128,128]{3,2,1,0:T(8,128)S(1)} %get-tuple-element.38), channel_id=1, source_target_pairs={{0,160},{32,192},{64,224},{96,0},{128,32},{160,64},{192,96},{224,1... | collective-permute-start | bytes 786440 | tf_op jit(solution)/shard_map/ppermute | solution.py:355
  92.0 1.5 %collective-permute-done.12.refs_3_ = f32[2,2,128,128]{3,2,1,0:T(8,128)S(1)} collective-permute-done((f32[2,2,128,128]{3,2,1,0:T(8,128)S(1)}, f32[2,2,128,128]{3,2,1,0:T(8,128)S(1)}, u32[]{:S(2)}, u32[]{:S(2)}) %collective-permute-start.12) | collective-permute-done | bytes 262176 | tf_op jit(solution)/shard_map/ppermute | solution.py:355
  93.5 0.5 collective-permute-start.7
  94.0 6.2 %all-to-all-done.2.got_ref = f32[16,8,2,2,8,128]{5,4,3,2,1,0:T(8,128)} async-done(((f32[16,8,2,2,8,128]{5,4,3,2,1,0:T(8,128)}), f32[16,8,2,2,8,128]{5,4,3,2,1,0:T(8,128)}, u32[]{:S(2)}, u32[]{:S(2)}) %all-to-all-start.2) | async-done | bytes 2097184 | tf_op jit(solution)/shard_map/all_to_all | solution.py:359
  100.1 3.1 %place_rows.1.refs_5_ = f32[8,2,2,2,128,128]{5,4,3,2,1,0:T(8,128)} custom-call(s32[8]{0:T(128)} %get-tuple-element.28.groups_ref, s32[8]{0:T(128)} %get-tuple-element.29.present_ref, f32[16,8,2,2,8,128]{5,4,3,2,1,0:T(8,128)} %all-to-all-done.2.got_ref), custom_call_target="tpu_custom_call" | custom-call | tf_op jit(solution)/shard_map/place_rows/pallas_call | solution.py:295
  103.2 0.0 copy-done.1
  103.3 0.0 copy-done.2
  103.3 8.3 %collective-permute-done.11.refs_2_ = f32[2,2,128,128]{3,2,1,0:T(8,128)S(1)} collective-permute-done((f32[2,2,128,128]{3,2,1,0:T(8,128)S(1)}, f32[2,2,128,128]{3,2,1,0:T(8,128)S(1)}, u32[]{:S(2)}, u32[]{:S(2)}) %collective-permute-start.11) | collective-permute-done | bytes 262176 | tf_op jit(solution)/shard_map/ppermute | solution.py:355
  111.6 0.0 collective-permute-done.10.refs_1_
  111.6 0.7 copy-done.4
  112.3 0.1 copy-done.5
  112.4 2.4 %place_blocks.2.refs_3_ = f32[8,2,2,2,128,128]{5,4,3,2,1,0:T(8,128)} custom-call(s32[8]{0:T(128)} %get-tuple-element.28.groups_ref, s32[8]{0:T(128)} %get-tuple-element.29.present_ref, f32[2,2,128,128]{3,2,1,0:T(8,128)} %get-tuple-element.36.refs_0_, f32[2,2,128,128]{3,2,1,0:T(8,128)} %copy-done.5, ...), custom_call_target="tpu_custom_call", output_to_operand_aliasing={{}: (7, {})} | custom-call | tf_op jit(solution)/shard_map/place_blocks/pallas_call | solution.py:334
  114.8 0.0 collective-permute-done.9.refs_2_
  114.8 0.0 copy-start
  114.8 6.1 %collective-permute-done.8.refs_1_ = f32[2,2,128,128]{3,2,1,0:T(8,128)S(1)} collective-permute-done((f32[2,2,128,128]{3,2,1,0:T(8,128)S(1)}, f32[2,2,128,128]{3,2,1,0:T(8,128)S(1)}, u32[]{:S(2)}, u32[]{:S(2)}) %collective-permute-start.8) | collective-permute-done | bytes 262176 | tf_op jit(solution)/shard_map/ppermute | solution.py:355
  120.9 3.5 %collective-permute-done.7.refs_0_ = f32[2,2,128,128]{3,2,1,0:T(8,128)S(1)} collective-permute-done((f32[2,2,128,128]{3,2,1,0:T(8,128)S(1)}, f32[2,2,128,128]{3,2,1,0:T(8,128)S(1)}, u32[]{:S(2)}, u32[]{:S(2)}) %collective-permute-start.7) | collective-permute-done | bytes 262176 | tf_op jit(solution)/shard_map/ppermute | solution.py:355
  124.4 0.0 copy-done
  124.4 0.0 copy-done.3
  124.4 0.7 copy-done.6
  125.1 2.0 %place_blocks.3 = f32[8,2,2,2,128,128]{5,4,3,2,1,0:T(8,128)} custom-call(s32[8]{0:T(128)} %get-tuple-element.28.groups_ref, s32[8]{0:T(128)} %get-tuple-element.29.present_ref, f32[2,2,128,128]{3,2,1,0:T(8,128)} %copy-done.6, f32[2,2,128,128]{3,2,1,0:T(8,128)} %copy-done.3, f32[2,2,128,128]{3,2,1,0:T(8,128)} %copy-done, ...), custom_call_target="tpu_custom_call", output_to_operand_aliasing={{}: (5, {})} | custom-call | tf_op jit(solution)/shard_map/place_blocks/pallas_call | solution.py:334
  (8 shorter events, 0.0 us)
Async XLA Ops:
  5.3 23.1 %all-to-all-start = ((f32[16,13,8,128]{3,2,1,0:T(8,128)}), f32[16,13,8,128]{3,2,1,0:T(8,128)S(1)}, u32[]{:S(2)}, u32[]{:S(2)}) async-start(f32[16,13,8,128]{3,2,1,0:T(8,128)} %span_states.3), calls=%async_computation | async-start | bytes 1703936 | tf_op jit(solution)/shard_map/all_to_all | solution.py:359
  28.5 38.0 %all-to-all-start.1 = ((f32[16,2,128,128]{3,2,1,0:T(8,128)}), f32[16,2,128,128]{3,2,1,0:T(8,128)S(1)}, u32[]{:S(2)}, u32[]{:S(2)}) async-start(f32[16,2,128,128]{3,2,1,0:T(8,128)} %span_states.2), calls=%async_computation.1 | async-start | bytes 4194304 | tf_op jit(solution)/shard_map/all_to_all | solution.py:359
  36.4 13.9 %collective-permute-start.6 = (f32[2,13,8,128]{3,2,1,0:T(8,128)S(1)}, f32[2,13,8,128]{3,2,1,0:T(8,128)S(1)}, u32[]{:S(2)}, u32[]{:S(2)}) collective-permute-start(f32[2,13,8,128]{3,2,1,0:T(8,128)S(1)} %get-tuple-element.40), channel_id=1, source_target_pairs={{0,128},{32,160},{64,192},{96,224},{128,0},{160,32},{192,64},{224,... | collective-permute-start | bytes 319496 | tf_op jit(solution)/shard_map/ppermute | solution.py:355
  43.6 11.7 %collective-permute-start.5 = (f32[2,13,8,128]{3,2,1,0:T(8,128)S(1)}, f32[2,13,8,128]{3,2,1,0:T(8,128)S(1)}, u32[]{:S(2)}, u32[]{:S(2)}) collective-permute-start(f32[2,13,8,128]{3,2,1,0:T(8,128)S(1)} %get-tuple-element.41), channel_id=1, source_target_pairs={{0,160},{32,192},{64,224},{96,0},{128,32},{160,64},{192,96},{224,1... | collective-permute-start | bytes 319496 | tf_op jit(solution)/shard_map/ppermute | solution.py:355
  43.6 16.0 %collective-permute-start.4 = (f32[2,13,8,128]{3,2,1,0:T(8,128)S(1)}, f32[2,13,8,128]{3,2,1,0:T(8,128)S(1)}, u32[]{:S(2)}, u32[]{:S(2)}) collective-permute-start(f32[2,13,8,128]{3,2,1,0:T(8,128)S(1)} %get-tuple-element.42), channel_id=1, source_target_pairs={{0,96},{32,128},{64,160},{96,192},{128,224},{160,0},{192,32},{224,... | collective-permute-start | bytes 319496 | tf_op jit(solution)/shard_map/ppermute | solution.py:355
  47.4 12.5 %collective-permute-start.3 = (f32[2,13,8,128]{3,2,1,0:T(8,128)S(1)}, f32[2,13,8,128]{3,2,1,0:T(8,128)S(1)}, u32[]{:S(2)}, u32[]{:S(2)}) collective-permute-start(f32[2,13,8,128]{3,2,1,0:T(8,128)S(1)} %get-tuple-element.43), channel_id=1, source_target_pairs={{0,192},{32,224},{64,0},{96,32},{128,64},{160,96},{192,128},{224,1... | collective-permute-start | bytes 319496 | tf_op jit(solution)/shard_map/ppermute | solution.py:355
  48.3 11.6 %collective-permute-start.2 = (f32[2,13,8,128]{3,2,1,0:T(8,128)S(1)}, f32[2,13,8,128]{3,2,1,0:T(8,128)S(1)}, u32[]{:S(2)}, u32[]{:S(2)}) collective-permute-start(f32[2,13,8,128]{3,2,1,0:T(8,128)S(1)} %get-tuple-element.44), channel_id=1, source_target_pairs={{0,64},{32,96},{64,128},{96,160},{128,192},{160,224},{192,0},{224,... | collective-permute-start | bytes 319496 | tf_op jit(solution)/shard_map/ppermute | solution.py:355
  50.3 11.9 %copy-start.7 = (f32[2,13,8,128]{3,2,1,0:T(8,128)}, f32[2,13,8,128]{3,2,1,0:T(8,128)S(1)}, u32[]{:S(2)}) copy-start(f32[2,13,8,128]{3,2,1,0:T(8,128)S(1)} %collective-permute-done.6.refs_7_) | copy-start | bytes 319492
  50.3 11.8 %collective-permute-start.1 = (f32[2,13,8,128]{3,2,1,0:T(8,128)S(1)}, f32[2,13,8,128]{3,2,1,0:T(8,128)S(1)}, u32[]{:S(2)}, u32[]{:S(2)}) collective-permute-start(f32[2,13,8,128]{3,2,1,0:T(8,128)S(1)} %get-tuple-element.45), channel_id=1, source_target_pairs={{0,224},{32,0},{64,32},{96,64},{128,96},{160,128},{192,160},{224,1... | collective-permute-start | bytes 319496 | tf_op jit(solution)/shard_map/ppermute | solution.py:355
  55.2 7.0 %copy-start.8 = (f32[2,13,8,128]{3,2,1,0:T(8,128)}, f32[2,13,8,128]{3,2,1,0:T(8,128)S(1)}, u32[]{:S(2)}) copy-start(f32[2,13,8,128]{3,2,1,0:T(8,128)S(1)} %collective-permute-done.5.refs_6_) | copy-start | bytes 319492
  55.2 6.9 %collective-permute-start = (f32[2,13,8,128]{3,2,1,0:T(8,128)S(1)}, f32[2,13,8,128]{3,2,1,0:T(8,128)S(1)}, u32[]{:S(2)}, u32[]{:S(2)}) collective-permute-start(f32[2,13,8,128]{3,2,1,0:T(8,128)S(1)} %get-tuple-element.46), channel_id=1, source_target_pairs={{0,32},{32,64},{64,96},{96,128},{128,160},{160,192},{192,224},{224... | collective-permute-start | bytes 319496 | tf_op jit(solution)/shard_map/ppermute | solution.py:355
  59.6 2.6 %copy-start.9 = (f32[2,13,8,128]{3,2,1,0:T(8,128)}, f32[2,13,8,128]{3,2,1,0:T(8,128)S(1)}, u32[]{:S(2)}) copy-start(f32[2,13,8,128]{3,2,1,0:T(8,128)S(1)} %collective-permute-done.4.refs_5_) | copy-start | bytes 319492
  59.9 2.3 %copy-start.10 = (f32[2,13,8,128]{3,2,1,0:T(8,128)}, f32[2,13,8,128]{3,2,1,0:T(8,128)S(1)}, u32[]{:S(2)}) copy-start(f32[2,13,8,128]{3,2,1,0:T(8,128)S(1)} %collective-permute-done.3.refs_4_) | copy-start | bytes 319492
  59.9 2.3 %copy-start.11 = (f32[2,13,8,128]{3,2,1,0:T(8,128)}, f32[2,13,8,128]{3,2,1,0:T(8,128)S(1)}, u32[]{:S(2)}) copy-start(f32[2,13,8,128]{3,2,1,0:T(8,128)S(1)} %collective-permute-done.2.refs_3_) | copy-start | bytes 319492
  62.2 0.7 copy-start.12
  62.2 0.7 copy-start.13
  66.5 33.6 %all-to-all-start.2 = ((f32[16,8,2,2,8,128]{5,4,3,2,1,0:T(8,128)}), f32[16,8,2,2,8,128]{5,4,3,2,1,0:T(8,128)}, u32[]{:S(2)}, u32[]{:S(2)}) async-start(f32[16,8,2,2,8,128]{5,4,3,2,1,0:T(8,128)} %get-tuple-element.31), calls=%async_computation.2 | async-start | bytes 4194304 | tf_op jit(solution)/shard_map/all_to_all | solution.py:359
  74.6 14.3 %collective-permute-start.13 = (f32[2,2,128,128]{3,2,1,0:T(8,128)S(1)}, f32[2,2,128,128]{3,2,1,0:T(8,128)S(1)}, u32[]{:S(2)}, u32[]{:S(2)}) collective-permute-start(f32[2,2,128,128]{3,2,1,0:T(8,128)S(1)} %get-tuple-element.32), channel_id=1, source_target_pairs={{0,192},{32,224},{64,0},{96,32},{128,64},{160,96},{192,128},{224,1... | collective-permute-start | bytes 786440 | tf_op jit(solution)/shard_map/ppermute | solution.py:355
  78.0 15.4 %collective-permute-start.12 = (f32[2,2,128,128]{3,2,1,0:T(8,128)S(1)}, f32[2,2,128,128]{3,2,1,0:T(8,128)S(1)}, u32[]{:S(2)}, u32[]{:S(2)}) collective-permute-start(f32[2,2,128,128]{3,2,1,0:T(8,128)S(1)} %get-tuple-element.33), channel_id=1, source_target_pairs={{0,64},{32,96},{64,128},{96,160},{128,192},{160,224},{192,0},{224,... | collective-permute-start | bytes 786440 | tf_op jit(solution)/shard_map/ppermute | solution.py:355
  78.0 33.5 %collective-permute-start.11 = (f32[2,2,128,128]{3,2,1,0:T(8,128)S(1)}, f32[2,2,128,128]{3,2,1,0:T(8,128)S(1)}, u32[]{:S(2)}, u32[]{:S(2)}) collective-permute-start(f32[2,2,128,128]{3,2,1,0:T(8,128)S(1)} %get-tuple-element.34), channel_id=1, source_target_pairs={{0,224},{32,0},{64,32},{96,64},{128,96},{160,128},{192,160},{224,1... | collective-permute-start | bytes 786440 | tf_op jit(solution)/shard_map/ppermute | solution.py:355
  81.1 30.5 %collective-permute-start.10 = (f32[2,2,128,128]{3,2,1,0:T(8,128)S(1)}, f32[2,2,128,128]{3,2,1,0:T(8,128)S(1)}, u32[]{:S(2)}, u32[]{:S(2)}) collective-permute-start(f32[2,2,128,128]{3,2,1,0:T(8,128)S(1)} %get-tuple-element.35), channel_id=1, source_target_pairs={{0,32},{32,64},{64,96},{96,128},{128,160},{160,192},{192,224},{224... | collective-permute-start | bytes 786440 | tf_op jit(solution)/shard_map/ppermute | solution.py:355
  81.1 33.6 %collective-permute-start.9 = (f32[2,2,128,128]{3,2,1,0:T(8,128)S(1)}, f32[2,2,128,128]{3,2,1,0:T(8,128)S(1)}, u32[]{:S(2)}, u32[]{:S(2)}) collective-permute-start(f32[2,2,128,128]{3,2,1,0:T(8,128)S(1)} %get-tuple-element.37), channel_id=1, source_target_pairs={{0,128},{32,160},{64,192},{96,224},{128,0},{160,32},{192,64},{224,... | collective-permute-start | bytes 786440 | tf_op jit(solution)/shard_map/ppermute | solution.py:355
  89.0 14.3 %copy-start.1 = (f32[2,2,128,128]{3,2,1,0:T(8,128)}, f32[2,2,128,128]{3,2,1,0:T(8,128)S(1)}, u32[]{:S(2)}) copy-start(f32[2,2,128,128]{3,2,1,0:T(8,128)S(1)} %collective-permute-done.13.refs_4_) | copy-start | bytes 786436
  89.0 31.9 %collective-permute-start.8 = (f32[2,2,128,128]{3,2,1,0:T(8,128)S(1)}, f32[2,2,128,128]{3,2,1,0:T(8,128)S(1)}, u32[]{:S(2)}, u32[]{:S(2)}) collective-permute-start(f32[2,2,128,128]{3,2,1,0:T(8,128)S(1)} %get-tuple-element.38), channel_id=1, source_target_pairs={{0,160},{32,192},{64,224},{96,0},{128,32},{160,64},{192,96},{224,1... | collective-permute-start | bytes 786440 | tf_op jit(solution)/shard_map/ppermute | solution.py:355
  93.5 9.8 %copy-start.2 = (f32[2,2,128,128]{3,2,1,0:T(8,128)}, f32[2,2,128,128]{3,2,1,0:T(8,128)S(1)}, u32[]{:S(2)}) copy-start(f32[2,2,128,128]{3,2,1,0:T(8,128)S(1)} %collective-permute-done.12.refs_3_) | copy-start | bytes 786436
  93.5 31.0 %collective-permute-start.7 = (f32[2,2,128,128]{3,2,1,0:T(8,128)S(1)}, f32[2,2,128,128]{3,2,1,0:T(8,128)S(1)}, u32[]{:S(2)}, u32[]{:S(2)}) collective-permute-start(f32[2,2,128,128]{3,2,1,0:T(8,128)S(1)} %get-tuple-element.39), channel_id=1, source_target_pairs={{0,96},{32,128},{64,160},{96,192},{128,224},{160,0},{192,32},{224,... | collective-permute-start | bytes 786440 | tf_op jit(solution)/shard_map/ppermute | solution.py:355
  111.6 0.7 copy-start.4
  111.6 0.8 copy-start.5
  114.8 9.6 %copy-start = (f32[2,2,128,128]{3,2,1,0:T(8,128)}, f32[2,2,128,128]{3,2,1,0:T(8,128)S(1)}, u32[]{:S(2)}) copy-start(f32[2,2,128,128]{3,2,1,0:T(8,128)S(1)} %collective-permute-done.9.refs_2_) | copy-start | bytes 786436
  120.9 3.5 %copy-start.3 = (f32[2,2,128,128]{3,2,1,0:T(8,128)}, f32[2,2,128,128]{3,2,1,0:T(8,128)S(1)}, u32[]{:S(2)}) copy-start(f32[2,2,128,128]{3,2,1,0:T(8,128)S(1)} %collective-permute-done.8.refs_1_) | copy-start | bytes 786436
  124.4 0.7 copy-start.6

commit v4 on v3

--- a/solution.py
+++ b/solution.py
@@ -369,14 +369,15 @@
     where = jnp.stack([lax.axis_index("pre"), lax.axis_index("dec")]).astype(jnp.int32)
     mixed = over_dec(span_states(True, 0, per, *spans))
     named = span_states(False, per, per, *spans)
-    prefill_out = span_output(lengths, queries, keys, values, ld, prior_state)
-    named, mixed, prefill_out, where = lax.optimization_barrier((named, mixed, prefill_out, where))
+    named, mixed, where = lax.optimization_barrier((named, mixed, where))
     owned = over_dec(named)
     held = [shifted(mixed, m, n_pre) for m in ORDER]
     blocks = [shifted(owned, m, n_pre) for m in ORDER]
     held, blocks[:FIRST] = lax.optimization_barrier((held, blocks[:FIRST]))
     sent, groups, present = address(where, held, n_dec, per)
     got = over_dec(sent)
+    got, queries = lax.optimization_barrier((got, queries))
+    prefill_out = span_output(lengths, queries, keys, values, ld, prior_state)
     decode_state = place_rows(groups, present, got, n_pre)
     decode_state = place_blocks(0, groups, present, blocks[:LATE], decode_state)
     decode_state = place_blocks(LATE, groups, present, blocks[LATE:], decode_state)

time: 128 us -> 124 us (0.969)
  waiting for transfers between devices: 35.4 us -> 29.7 us
    ppermute x14, waiting for transfers between devices: 29.2 us -> 19.8 us  [shifted(): lax.ppermute(part, 'pre', [(i, (i + shift) % n_pre) for i in range(n_pre)])]
    all_to_all x3, waiting for transfers between devices: 6.18 us -> 9.85 us  [over_dec(): return lax.all_to_all(x, 'dec', split_axis=0, concat_axis=0, tiled=True)]
    ppermute x14, starting transfers between devices: 33.8 us -> 36.8 us  [shifted(): lax.ppermute(part, 'pre', [(i, (i + shift) % n_pre) for i in range(n_pre)])]
    all_to_all x3, starting transfers between devices: 21.9 us -> 20 us  [over_dec(): return lax.all_to_all(x, 'dec', split_axis=0, concat_axis=0, tiled=True)]
  transfers between devices with their start and end apart: 17 -> 17, of which waited for: 9 -> 8; matrix products, arithmetic and copies ran while one was open for 2% -> 2% of each run, Pallas kernels for 19% -> 20%
where the time goes in v4:
time: 124 us; the launch traced here: 122 us
  starting transfers between devices  56.8 us (46%)
  Pallas kernels  30.7 us (25%)
  waiting for transfers between devices  29.7 us (24%)
  local copies, waits for them, and re-layouts  3.62 us (3%)
    ppermute x14, starting transfers between devices, shifted(): lax.ppermute(part, 'pre', [(i, (i + shift) % n_pre) for i in range(n_pre)])  36.8 us
    all_to_all x3, starting transfers between devices, over_dec(): return lax.all_to_all(x, 'dec', split_axis=0, concat_axis=0, tiled=True)  20 us
    ppermute x14, waiting for transfers between devices, shifted(): lax.ppermute(part, 'pre', [(i, (i + shift) % n_pre) for i in range(n_pre)])  19.8 us
    pallas_call x1, Pallas kernels, span_output(): pl.pallas_call(output_kernel, grid_spec=pltpu.PrefetchScalarGridSpec(num_...  9.88 us
    all_to_all x3, waiting for transfers between devices, over_dec(): return lax.all_to_all(x, 'dec', split_axis=0, concat_axis=0, tiled=True)  9.85 us
    pallas_call x2, Pallas kernels, span_states(): pl.pallas_call(functools.partial(mixing_kernel if mixing else owner_kerne...  9.83 us
    pallas_call x2, Pallas kernels, place_blocks(): pl.pallas_call(functools.partial(place_blocks_kernel, first, slots), in_s...  4.41 us
    pallas_call x1, Pallas kernels, address(): pl.pallas_call(functools.partial(address_kernel, slots, len(ORDER)), in_s...  3.6 us
  transfers between devices with their start and end apart: 17, of which 8 were waited for; matrix products, arithmetic and copies ran while one was open for 2% of the time, Pallas kernels for 20%

profile of v4, /device:TPU:2, one launch (start us, length us, event | category | flops | bytes accessed | tf_op | source)
XLA Modules:
  0.0 122.2 jit_solution(13121077796997416908)
XLA Ops:
  0.6 4.7 %span_states.3 = f32[16,13,8,128]{3,2,1,0:T(8,128)} custom-call(s32[6]{0:T(128)} %lengths_ref.5, s32[6]{0:T(128)} %bitcast.9, bf16[6,256,512]{2,1,0:T(8,128)(2,1)} %k_ref.5, bf16[6,256,512]{2,1,0:T(8,128)(2,1)} %v_ref.5, f32[6,4,256]{2,1,0:T(4,128)} %bitcast.6, f32[6,4,128,128]{3,2,1,0:T(8,128)} %prior_ref.5), custom_call_target="tpu_custom_call" | custom-call | flops 100663296 | bytes 3145728 | tf_op jit(solution)/shard_map/span_states/pallas_call | solution.py:124
  5.3 7.5 %all-to-all-start = ((f32[16,13,8,128]{3,2,1,0:T(8,128)}), f32[16,13,8,128]{3,2,1,0:T(8,128)S(1)}, u32[]{:S(2)}, u32[]{:S(2)}) async-start(f32[16,13,8,128]{3,2,1,0:T(8,128)} %span_states.3), calls=%async_computation | async-start | bytes 1703936 | tf_op jit(solution)/shard_map/all_to_all | solution.py:359
  12.8 5.1 %span_states.2 = f32[16,2,128,128]{3,2,1,0:T(8,128)} custom-call(s32[6]{0:T(128)} %lengths_ref.5, s32[6]{0:T(128)} %bitcast.10, bf16[6,256,512]{2,1,0:T(8,128)(2,1)} %k_ref.5, bf16[6,256,512]{2,1,0:T(8,128)(2,1)} %v_ref.5, f32[6,4,256]{2,1,0:T(4,128)} %bitcast.7, f32[6,4,128,128]{3,2,1,0:T(8,128)} %prior_ref.5), custom_call_target="tpu_custom_call" | custom-call | flops 100663296 | bytes 3145728 | tf_op jit(solution)/shard_map/span_states/pallas_call | solution.py:124
  17.9 0.6 pad_add_fusion.where_ref
  18.5 8.0 %all-to-all-done = f32[16,13,8,128]{3,2,1,0:T(8,128)S(1)} async-done(((f32[16,13,8,128]{3,2,1,0:T(8,128)}), f32[16,13,8,128]{3,2,1,0:T(8,128)S(1)}, u32[]{:S(2)}, u32[]{:S(2)}) %all-to-all-start) | async-done | bytes 852000 | tf_op jit(solution)/shard_map/all_to_all | solution.py:359
  26.5 5.1 %all-to-all-start.2 = ((f32[16,2,128,128]{3,2,1,0:T(8,128)}), f32[16,2,128,128]{3,2,1,0:T(8,128)S(1)}, u32[]{:S(2)}, u32[]{:S(2)}) async-start(f32[16,2,128,128]{3,2,1,0:T(8,128)} %span_states.2), calls=%async_computation.2 | async-start | bytes 4194304 | tf_op jit(solution)/shard_map/all_to_all | solution.py:359
  31.7 0.7 constant_dynamic-slice_fusion.8
  32.4 1.9 %collective-permute-start = (f32[2,13,8,128]{3,2,1,0:T(8,128)S(1)}, f32[2,13,8,128]{3,2,1,0:T(8,128)S(1)}, u32[]{:S(2)}, u32[]{:S(2)}) collective-permute-start(f32[2,13,8,128]{3,2,1,0:T(8,128)S(1)} %get-tuple-element.48), channel_id=1, source_target_pairs={{0,32},{32,64},{64,96},{96,128},{128,160},{160,192},{192,224},{224... | collective-permute-start | bytes 319496 | tf_op jit(solution)/shard_map/ppermute | solution.py:355
  34.3 3.9 %collective-permute-start.1 = (f32[2,13,8,128]{3,2,1,0:T(8,128)S(1)}, f32[2,13,8,128]{3,2,1,0:T(8,128)S(1)}, u32[]{:S(2)}, u32[]{:S(2)}) collective-permute-start(f32[2,13,8,128]{3,2,1,0:T(8,128)S(1)} %get-tuple-element.47), channel_id=1, source_target_pairs={{0,224},{32,0},{64,32},{96,64},{128,96},{160,128},{192,160},{224,1... | collective-permute-start | bytes 319496 | tf_op jit(solution)/shard_map/ppermute | solution.py:355
  38.2 0.0 collective-permute-start.2
  38.2 4.1 %collective-permute-start.3 = (f32[2,13,8,128]{3,2,1,0:T(8,128)S(1)}, f32[2,13,8,128]{3,2,1,0:T(8,128)S(1)}, u32[]{:S(2)}, u32[]{:S(2)}) collective-permute-start(f32[2,13,8,128]{3,2,1,0:T(8,128)S(1)} %get-tuple-element.45), channel_id=1, source_target_pairs={{0,192},{32,224},{64,0},{96,32},{128,64},{160,96},{192,128},{224,1... | collective-permute-start | bytes 319496 | tf_op jit(solution)/shard_map/ppermute | solution.py:355
  42.4 0.7 collective-permute-start.4
  43.1 0.0 collective-permute-done.refs_1_
  43.1 0.0 copy-start.7
  43.1 4.3 %collective-permute-start.5 = (f32[2,13,8,128]{3,2,1,0:T(8,128)S(1)}, f32[2,13,8,128]{3,2,1,0:T(8,128)S(1)}, u32[]{:S(2)}, u32[]{:S(2)}) collective-permute-start(f32[2,13,8,128]{3,2,1,0:T(8,128)S(1)} %get-tuple-element.43), channel_id=1, source_target_pairs={{0,160},{32,192},{64,224},{96,0},{128,32},{160,64},{192,96},{224,1... | collective-permute-start | bytes 319496 | tf_op jit(solution)/shard_map/ppermute | solution.py:355
  47.4 0.0 collective-permute-done.1.refs_2_
  47.4 0.0 copy-start.8
  47.4 4.6 %collective-permute-start.6 = (f32[2,13,8,128]{3,2,1,0:T(8,128)S(1)}, f32[2,13,8,128]{3,2,1,0:T(8,128)S(1)}, u32[]{:S(2)}, u32[]{:S(2)}) collective-permute-start(f32[2,13,8,128]{3,2,1,0:T(8,128)S(1)} %get-tuple-element.42), channel_id=1, source_target_pairs={{0,128},{32,160},{64,192},{96,224},{128,0},{160,32},{192,64},{224,... | collective-permute-start | bytes 319496 | tf_op jit(solution)/shard_map/ppermute | solution.py:355
  52.0 0.0 collective-permute-done.2.refs_3_
  52.0 0.0 copy-start.9
  52.0 0.0 collective-permute-done.3.refs_4_
  52.0 0.0 copy-start.10
  52.0 2.6 %collective-permute-done.4.refs_5_ = f32[2,13,8,128]{3,2,1,0:T(8,128)S(1)} collective-permute-done((f32[2,13,8,128]{3,2,1,0:T(8,128)S(1)}, f32[2,13,8,128]{3,2,1,0:T(8,128)S(1)}, u32[]{:S(2)}, u32[]{:S(2)}) %collective-permute-start.4) | collective-permute-done | bytes 106528 | tf_op jit(solution)/shard_map/ppermute | solution.py:355
  54.6 0.0 copy-start.11
  54.6 0.0 collective-permute-done.5.refs_6_
  54.6 0.0 copy-start.12
  54.6 2.6 %collective-permute-done.6.refs_7_ = f32[2,13,8,128]{3,2,1,0:T(8,128)S(1)} collective-permute-done((f32[2,13,8,128]{3,2,1,0:T(8,128)S(1)}, f32[2,13,8,128]{3,2,1,0:T(8,128)S(1)}, u32[]{:S(2)}, u32[]{:S(2)}) %collective-permute-start.6) | collective-permute-done | bytes 106528 | tf_op jit(solution)/shard_map/ppermute | solution.py:355
  57.3 0.0 copy-done.7
  57.3 0.0 copy-done.8
  57.3 0.0 copy-done.9
  57.3 0.0 copy-done.10
  57.3 0.0 copy-done.11
  57.3 0.0 copy-done.12
  57.3 0.6 copy-done.13
  57.9 3.6 %address.1 = (f32[16,8,2,2,8,128]{5,4,3,2,1,0:T(8,128)}, s32[8]{0:T(128)}, s32[8]{0:T(128)}) custom-call(s32[2]{0:T(128)} %pad_add_fusion.where_ref, f32[2,13,8,128]{3,2,1,0:T(8,128)} %get-tuple-element.20.refs_0_, f32[2,13,8,128]{3,2,1,0:T(8,128)} %copy-done.7, f32[2,13,8,128]{3,2,1,0:T(8,128)} %copy-done.8, f32[2,13,8,128]{3,2,1,0:T(8,128)} %copy-done.9, ...), custom_call_target="tpu_custom_call" | custom-call | tf_op jit(solution)/shard_map/address/pallas_call | solution.py:241
  61.5 0.0 all-to-all-done.2
  61.5 7.4 %all-to-all-start.1 = ((f32[16,8,2,2,8,128]{5,4,3,2,1,0:T(8,128)}), f32[16,8,2,2,8,128]{5,4,3,2,1,0:T(8,128)}, u32[]{:S(2)}, u32[]{:S(2)}) async-start(f32[16,8,2,2,8,128]{5,4,3,2,1,0:T(8,128)} %get-tuple-element.28), calls=%async_computation.1 | async-start | bytes 4194304 | tf_op jit(solution)/shard_map/all_to_all | solution.py:359
  68.9 0.9 constant_dynamic-slice_fusion
  69.8 5.0 %collective-permute-start.10 = (f32[2,2,128,128]{3,2,1,0:T(8,128)S(1)}, f32[2,2,128,128]{3,2,1,0:T(8,128)S(1)}, u32[]{:S(2)}, u32[]{:S(2)}) collective-permute-start(f32[2,2,128,128]{3,2,1,0:T(8,128)S(1)} %get-tuple-element.37), channel_id=1, source_target_pairs={{0,32},{32,64},{64,96},{96,128},{128,160},{160,192},{192,224},{224... | collective-permute-start | bytes 786440 | tf_op jit(solution)/shard_map/ppermute | solution.py:355
  74.8 0.0 collective-permute-start.11
  74.8 1.5 %collective-permute-start.12 = (f32[2,2,128,128]{3,2,1,0:T(8,128)S(1)}, f32[2,2,128,128]{3,2,1,0:T(8,128)S(1)}, u32[]{:S(2)}, u32[]{:S(2)}) collective-permute-start(f32[2,2,128,128]{3,2,1,0:T(8,128)S(1)} %get-tuple-element.35), channel_id=1, source_target_pairs={{0,64},{32,96},{64,128},{96,160},{128,192},{160,224},{192,0},{224,... | collective-permute-start | bytes 786440 | tf_op jit(solution)/shard_map/ppermute | solution.py:355
  76.3 2.7 %collective-permute-start.13 = (f32[2,2,128,128]{3,2,1,0:T(8,128)S(1)}, f32[2,2,128,128]{3,2,1,0:T(8,128)S(1)}, u32[]{:S(2)}, u32[]{:S(2)}) collective-permute-start(f32[2,2,128,128]{3,2,1,0:T(8,128)S(1)} %get-tuple-element.34), channel_id=1, source_target_pairs={{0,192},{32,224},{64,0},{96,32},{128,64},{160,96},{192,128},{224,1... | collective-permute-start | bytes 786440 | tf_op jit(solution)/shard_map/ppermute | solution.py:355
  78.9 0.3 collective-permute-start.7
  79.2 5.0 %collective-permute-done.10.refs_1_ = f32[2,2,128,128]{3,2,1,0:T(8,128)S(1)} collective-permute-done((f32[2,2,128,128]{3,2,1,0:T(8,128)S(1)}, f32[2,2,128,128]{3,2,1,0:T(8,128)S(1)}, u32[]{:S(2)}, u32[]{:S(2)}) %collective-permute-start.10) | collective-permute-done | bytes 262176 | tf_op jit(solution)/shard_map/ppermute | solution.py:355
  84.2 1.4 %collective-permute-start.8 = (f32[2,2,128,128]{3,2,1,0:T(8,128)S(1)}, f32[2,2,128,128]{3,2,1,0:T(8,128)S(1)}, u32[]{:S(2)}, u32[]{:S(2)}) collective-permute-start(f32[2,2,128,128]{3,2,1,0:T(8,128)S(1)} %get-tuple-element.40), channel_id=1, source_target_pairs={{0,160},{32,192},{64,224},{96,0},{128,32},{160,64},{192,96},{224,1... | collective-permute-start | bytes 786440 | tf_op jit(solution)/shard_map/ppermute | solution.py:355
  85.7 0.0 collective-permute-done.11.refs_2_
  85.7 6.4 %collective-permute-start.9 = (f32[2,2,128,128]{3,2,1,0:T(8,128)S(1)}, f32[2,2,128,128]{3,2,1,0:T(8,128)S(1)}, u32[]{:S(2)}, u32[]{:S(2)}) collective-permute-start(f32[2,2,128,128]{3,2,1,0:T(8,128)S(1)} %get-tuple-element.39), channel_id=1, source_target_pairs={{0,128},{32,160},{64,192},{96,224},{128,0},{160,32},{192,64},{224,... | collective-permute-start | bytes 786440 | tf_op jit(solution)/shard_map/ppermute | solution.py:355
  92.1 1.8 %all-to-all-done.1.got_ref = f32[16,8,2,2,8,128]{5,4,3,2,1,0:T(8,128)} async-done(((f32[16,8,2,2,8,128]{5,4,3,2,1,0:T(8,128)}), f32[16,8,2,2,8,128]{5,4,3,2,1,0:T(8,128)}, u32[]{:S(2)}, u32[]{:S(2)}) %all-to-all-start.1) | async-done | bytes 2097184 | tf_op jit(solution)/shard_map/all_to_all | solution.py:359
  93.9 3.0 %place_rows.1.refs_5_ = f32[8,2,2,2,128,128]{5,4,3,2,1,0:T(8,128)} custom-call(s32[8]{0:T(128)} %get-tuple-element.30.groups_ref, s32[8]{0:T(128)} %get-tuple-element.31.present_ref, f32[16,8,2,2,8,128]{5,4,3,2,1,0:T(8,128)} %all-to-all-done.1.got_ref), custom_call_target="tpu_custom_call" | custom-call | tf_op jit(solution)/shard_map/place_rows/pallas_call | solution.py:295
  96.9 0.0 copy-done.1
  96.9 0.0 copy-done.2
  96.9 9.9 %span_output.1 = bf16[6,256,512]{2,1,0:T(8,128)(2,1)} custom-call(s32[6]{0:T(128)} %lengths_ref.5, bf16[6,256,512]{2,1,0:T(8,128)(2,1)} %q_ref, bf16[6,256,512]{2,1,0:T(8,128)(2,1)} %k_ref.5, bf16[6,256,512]{2,1,0:T(8,128)(2,1)} %v_ref.5, f32[6,4,256]{2,1,0:T(4,128)} %bitcast.8, f32[6,4,128,128]{3,2,1,0:T(8,128)} %prior_ref.5), custom_call_target="tpu_custom_call" | custom-call | flops 1409286144 | bytes 7864320 | tf_op jit(solution)/shard_map/span_output/pallas_call | solution.py:187
  106.8 0.0 collective-permute-done.12.refs_3_
  106.8 0.1 collective-permute-done.13.refs_4_
  106.9 0.6 copy-done.4
  107.5 0.1 copy-done.5
  107.6 2.4 %place_blocks.2.refs_3_ = f32[8,2,2,2,128,128]{5,4,3,2,1,0:T(8,128)} custom-call(s32[8]{0:T(128)} %get-tuple-element.30.groups_ref, s32[8]{0:T(128)} %get-tuple-element.31.present_ref, f32[2,2,128,128]{3,2,1,0:T(8,128)} %get-tuple-element.38.refs_0_, f32[2,2,128,128]{3,2,1,0:T(8,128)} %copy-done.1, ...), custom_call_target="tpu_custom_call", output_to_operand_aliasing={{}: (7, {})} | custom-call | tf_op jit(solution)/shard_map/place_blocks/pallas_call | solution.py:334
  110.0 5.2 %collective-permute-done.7.refs_0_ = f32[2,2,128,128]{3,2,1,0:T(8,128)S(1)} collective-permute-done((f32[2,2,128,128]{3,2,1,0:T(8,128)S(1)}, f32[2,2,128,128]{3,2,1,0:T(8,128)S(1)}, u32[]{:S(2)}, u32[]{:S(2)}) %collective-permute-start.7) | collective-permute-done | bytes 262176 | tf_op jit(solution)/shard_map/ppermute | solution.py:355
  115.3 0.0 collective-permute-done.8.refs_1_
  115.3 4.2 %collective-permute-done.9.refs_2_ = f32[2,2,128,128]{3,2,1,0:T(8,128)S(1)} collective-permute-done((f32[2,2,128,128]{3,2,1,0:T(8,128)S(1)}, f32[2,2,128,128]{3,2,1,0:T(8,128)S(1)}, u32[]{:S(2)}, u32[]{:S(2)}) %collective-permute-start.9) | collective-permute-done | bytes 262176 | tf_op jit(solution)/shard_map/ppermute | solution.py:355
  119.5 0.0 copy-done
  119.5 0.0 copy-done.3
  119.5 0.7 copy-done.6
  120.2 2.0 %place_blocks.3 = f32[8,2,2,2,128,128]{5,4,3,2,1,0:T(8,128)} custom-call(s32[8]{0:T(128)} %get-tuple-element.30.groups_ref, s32[8]{0:T(128)} %get-tuple-element.31.present_ref, f32[2,2,128,128]{3,2,1,0:T(8,128)} %copy-done, f32[2,2,128,128]{3,2,1,0:T(8,128)} %copy-done.3, f32[2,2,128,128]{3,2,1,0:T(8,128)} %copy-done.6, ...), custom_call_target="tpu_custom_call", output_to_operand_aliasing={{}: (5, {})} | custom-call | tf_op jit(solution)/shard_map/place_blocks/pallas_call | solution.py:334
  (8 shorter events, 0.0 us)
Async XLA Ops:
  5.3 21.2 %all-to-all-start = ((f32[16,13,8,128]{3,2,1,0:T(8,128)}), f32[16,13,8,128]{3,2,1,0:T(8,128)S(1)}, u32[]{:S(2)}, u32[]{:S(2)}) async-start(f32[16,13,8,128]{3,2,1,0:T(8,128)} %span_states.3), calls=%async_computation | async-start | bytes 1703936 | tf_op jit(solution)/shard_map/all_to_all | solution.py:359
  26.5 35.0 %all-to-all-start.2 = ((f32[16,2,128,128]{3,2,1,0:T(8,128)}), f32[16,2,128,128]{3,2,1,0:T(8,128)S(1)}, u32[]{:S(2)}, u32[]{:S(2)}) async-start(f32[16,2,128,128]{3,2,1,0:T(8,128)} %span_states.2), calls=%async_computation.2 | async-start | bytes 4194304 | tf_op jit(solution)/shard_map/all_to_all | solution.py:359
  32.4 10.7 %collective-permute-start = (f32[2,13,8,128]{3,2,1,0:T(8,128)S(1)}, f32[2,13,8,128]{3,2,1,0:T(8,128)S(1)}, u32[]{:S(2)}, u32[]{:S(2)}) collective-permute-start(f32[2,13,8,128]{3,2,1,0:T(8,128)S(1)} %get-tuple-element.48), channel_id=1, source_target_pairs={{0,32},{32,64},{64,96},{96,128},{128,160},{160,192},{192,224},{224... | collective-permute-start | bytes 319496 | tf_op jit(solution)/shard_map/ppermute | solution.py:355
  34.3 13.1 %collective-permute-start.1 = (f32[2,13,8,128]{3,2,1,0:T(8,128)S(1)}, f32[2,13,8,128]{3,2,1,0:T(8,128)S(1)}, u32[]{:S(2)}, u32[]{:S(2)}) collective-permute-start(f32[2,13,8,128]{3,2,1,0:T(8,128)S(1)} %get-tuple-element.47), channel_id=1, source_target_pairs={{0,224},{32,0},{64,32},{96,64},{128,96},{160,128},{192,160},{224,1... | collective-permute-start | bytes 319496 | tf_op jit(solution)/shard_map/ppermute | solution.py:355
  38.2 13.8 %collective-permute-start.2 = (f32[2,13,8,128]{3,2,1,0:T(8,128)S(1)}, f32[2,13,8,128]{3,2,1,0:T(8,128)S(1)}, u32[]{:S(2)}, u32[]{:S(2)}) collective-permute-start(f32[2,13,8,128]{3,2,1,0:T(8,128)S(1)} %get-tuple-element.46), channel_id=1, source_target_pairs={{0,64},{32,96},{64,128},{96,160},{128,192},{160,224},{192,0},{224,... | collective-permute-start | bytes 319496 | tf_op jit(solution)/shard_map/ppermute | solution.py:355
  38.2 13.8 %collective-permute-start.3 = (f32[2,13,8,128]{3,2,1,0:T(8,128)S(1)}, f32[2,13,8,128]{3,2,1,0:T(8,128)S(1)}, u32[]{:S(2)}, u32[]{:S(2)}) collective-permute-start(f32[2,13,8,128]{3,2,1,0:T(8,128)S(1)} %get-tuple-element.45), channel_id=1, source_target_pairs={{0,192},{32,224},{64,0},{96,32},{128,64},{160,96},{192,128},{224,1... | collective-permute-start | bytes 319496 | tf_op jit(solution)/shard_map/ppermute | solution.py:355
  42.4 12.2 %collective-permute-start.4 = (f32[2,13,8,128]{3,2,1,0:T(8,128)S(1)}, f32[2,13,8,128]{3,2,1,0:T(8,128)S(1)}, u32[]{:S(2)}, u32[]{:S(2)}) collective-permute-start(f32[2,13,8,128]{3,2,1,0:T(8,128)S(1)} %get-tuple-element.44), channel_id=1, source_target_pairs={{0,96},{32,128},{64,160},{96,192},{128,224},{160,0},{192,32},{224,... | collective-permute-start | bytes 319496 | tf_op jit(solution)/shard_map/ppermute | solution.py:355
  43.1 14.2 %copy-start.7 = (f32[2,13,8,128]{3,2,1,0:T(8,128)}, f32[2,13,8,128]{3,2,1,0:T(8,128)S(1)}, u32[]{:S(2)}) copy-start(f32[2,13,8,128]{3,2,1,0:T(8,128)S(1)} %collective-permute-done.refs_1_) | copy-start | bytes 319492
  43.1 11.6 %collective-permute-start.5 = (f32[2,13,8,128]{3,2,1,0:T(8,128)S(1)}, f32[2,13,8,128]{3,2,1,0:T(8,128)S(1)}, u32[]{:S(2)}, u32[]{:S(2)}) collective-permute-start(f32[2,13,8,128]{3,2,1,0:T(8,128)S(1)} %get-tuple-element.43), channel_id=1, source_target_pairs={{0,160},{32,192},{64,224},{96,0},{128,32},{160,64},{192,96},{224,1... | collective-permute-start | bytes 319496 | tf_op jit(solution)/shard_map/ppermute | solution.py:355
  47.4 9.8 %copy-start.8 = (f32[2,13,8,128]{3,2,1,0:T(8,128)}, f32[2,13,8,128]{3,2,1,0:T(8,128)S(1)}, u32[]{:S(2)}) copy-start(f32[2,13,8,128]{3,2,1,0:T(8,128)S(1)} %collective-permute-done.1.refs_2_) | copy-start | bytes 319492
  47.4 9.8 %collective-permute-start.6 = (f32[2,13,8,128]{3,2,1,0:T(8,128)S(1)}, f32[2,13,8,128]{3,2,1,0:T(8,128)S(1)}, u32[]{:S(2)}, u32[]{:S(2)}) collective-permute-start(f32[2,13,8,128]{3,2,1,0:T(8,128)S(1)} %get-tuple-element.42), channel_id=1, source_target_pairs={{0,128},{32,160},{64,192},{96,224},{128,0},{160,32},{192,64},{224,... | collective-permute-start | bytes 319496 | tf_op jit(solution)/shard_map/ppermute | solution.py:355
  52.0 5.3 %copy-start.9 = (f32[2,13,8,128]{3,2,1,0:T(8,128)}, f32[2,13,8,128]{3,2,1,0:T(8,128)S(1)}, u32[]{:S(2)}) copy-start(f32[2,13,8,128]{3,2,1,0:T(8,128)S(1)} %collective-permute-done.2.refs_3_) | copy-start | bytes 319492
  52.0 5.3 %copy-start.10 = (f32[2,13,8,128]{3,2,1,0:T(8,128)}, f32[2,13,8,128]{3,2,1,0:T(8,128)S(1)}, u32[]{:S(2)}) copy-start(f32[2,13,8,128]{3,2,1,0:T(8,128)S(1)} %collective-permute-done.3.refs_4_) | copy-start | bytes 319492
  54.6 2.7 %copy-start.11 = (f32[2,13,8,128]{3,2,1,0:T(8,128)}, f32[2,13,8,128]{3,2,1,0:T(8,128)S(1)}, u32[]{:S(2)}) copy-start(f32[2,13,8,128]{3,2,1,0:T(8,128)S(1)} %collective-permute-done.4.refs_5_) | copy-start | bytes 319492
  54.6 2.7 %copy-start.12 = (f32[2,13,8,128]{3,2,1,0:T(8,128)}, f32[2,13,8,128]{3,2,1,0:T(8,128)S(1)}, u32[]{:S(2)}) copy-start(f32[2,13,8,128]{3,2,1,0:T(8,128)S(1)} %collective-permute-done.5.refs_6_) | copy-start | bytes 319492
  57.3 0.6 copy-start.13
  61.5 32.4 %all-to-all-start.1 = ((f32[16,8,2,2,8,128]{5,4,3,2,1,0:T(8,128)}), f32[16,8,2,2,8,128]{5,4,3,2,1,0:T(8,128)}, u32[]{:S(2)}, u32[]{:S(2)}) async-start(f32[16,8,2,2,8,128]{5,4,3,2,1,0:T(8,128)} %get-tuple-element.28), calls=%async_computation.1 | async-start | bytes 4194304 | tf_op jit(solution)/shard_map/all_to_all | solution.py:359
  69.8 14.5 %collective-permute-start.10 = (f32[2,2,128,128]{3,2,1,0:T(8,128)S(1)}, f32[2,2,128,128]{3,2,1,0:T(8,128)S(1)}, u32[]{:S(2)}, u32[]{:S(2)}) collective-permute-start(f32[2,2,128,128]{3,2,1,0:T(8,128)S(1)} %get-tuple-element.37), channel_id=1, source_target_pairs={{0,32},{32,64},{64,96},{96,128},{128,160},{160,192},{192,224},{224... | collective-permute-start | bytes 786440 | tf_op jit(solution)/shard_map/ppermute | solution.py:355
  74.8 10.9 %collective-permute-start.11 = (f32[2,2,128,128]{3,2,1,0:T(8,128)S(1)}, f32[2,2,128,128]{3,2,1,0:T(8,128)S(1)}, u32[]{:S(2)}, u32[]{:S(2)}) collective-permute-start(f32[2,2,128,128]{3,2,1,0:T(8,128)S(1)} %get-tuple-element.36), channel_id=1, source_target_pairs={{0,224},{32,0},{64,32},{96,64},{128,96},{160,128},{192,160},{224,1... | collective-permute-start | bytes 786440 | tf_op jit(solution)/shard_map/ppermute | solution.py:355
  74.8 32.0 %collective-permute-start.12 = (f32[2,2,128,128]{3,2,1,0:T(8,128)S(1)}, f32[2,2,128,128]{3,2,1,0:T(8,128)S(1)}, u32[]{:S(2)}, u32[]{:S(2)}) collective-permute-start(f32[2,2,128,128]{3,2,1,0:T(8,128)S(1)} %get-tuple-element.35), channel_id=1, source_target_pairs={{0,64},{32,96},{64,128},{96,160},{128,192},{160,224},{192,0},{224,... | collective-permute-start | bytes 786440 | tf_op jit(solution)/shard_map/ppermute | solution.py:355
  76.3 30.7 %collective-permute-start.13 = (f32[2,2,128,128]{3,2,1,0:T(8,128)S(1)}, f32[2,2,128,128]{3,2,1,0:T(8,128)S(1)}, u32[]{:S(2)}, u32[]{:S(2)}) collective-permute-start(f32[2,2,128,128]{3,2,1,0:T(8,128)S(1)} %get-tuple-element.34), channel_id=1, source_target_pairs={{0,192},{32,224},{64,0},{96,32},{128,64},{160,96},{192,128},{224,1... | collective-permute-start | bytes 786440 | tf_op jit(solution)/shard_map/ppermute | solution.py:355
  78.9 36.3 %collective-permute-start.7 = (f32[2,2,128,128]{3,2,1,0:T(8,128)S(1)}, f32[2,2,128,128]{3,2,1,0:T(8,128)S(1)}, u32[]{:S(2)}, u32[]{:S(2)}) collective-permute-start(f32[2,2,128,128]{3,2,1,0:T(8,128)S(1)} %get-tuple-element.41), channel_id=1, source_target_pairs={{0,96},{32,128},{64,160},{96,192},{128,224},{160,0},{192,32},{224,... | collective-permute-start | bytes 786440 | tf_op jit(solution)/shard_map/ppermute | solution.py:355
  84.2 12.7 %copy-start.1 = (f32[2,2,128,128]{3,2,1,0:T(8,128)}, f32[2,2,128,128]{3,2,1,0:T(8,128)S(1)}, u32[]{:S(2)}) copy-start(f32[2,2,128,128]{3,2,1,0:T(8,128)S(1)} %collective-permute-done.10.refs_1_) | copy-start | bytes 786436
  84.2 31.0 %collective-permute-start.8 = (f32[2,2,128,128]{3,2,1,0:T(8,128)S(1)}, f32[2,2,128,128]{3,2,1,0:T(8,128)S(1)}, u32[]{:S(2)}, u32[]{:S(2)}) collective-permute-start(f32[2,2,128,128]{3,2,1,0:T(8,128)S(1)} %get-tuple-element.40), channel_id=1, source_target_pairs={{0,160},{32,192},{64,224},{96,0},{128,32},{160,64},{192,96},{224,1... | collective-permute-start | bytes 786440 | tf_op jit(solution)/shard_map/ppermute | solution.py:355
  85.7 11.2 %copy-start.2 = (f32[2,2,128,128]{3,2,1,0:T(8,128)}, f32[2,2,128,128]{3,2,1,0:T(8,128)S(1)}, u32[]{:S(2)}) copy-start(f32[2,2,128,128]{3,2,1,0:T(8,128)S(1)} %collective-permute-done.11.refs_2_) | copy-start | bytes 786436
  85.7 33.8 %collective-permute-start.9 = (f32[2,2,128,128]{3,2,1,0:T(8,128)S(1)}, f32[2,2,128,128]{3,2,1,0:T(8,128)S(1)}, u32[]{:S(2)}, u32[]{:S(2)}) collective-permute-start(f32[2,2,128,128]{3,2,1,0:T(8,128)S(1)} %get-tuple-element.39), channel_id=1, source_target_pairs={{0,128},{32,160},{64,192},{96,224},{128,0},{160,32},{192,64},{224,... | collective-permute-start | bytes 786440 | tf_op jit(solution)/shard_map/ppermute | solution.py:355
  106.8 0.7 copy-start.4
  106.9 0.7 copy-start.5
  115.3 4.2 %copy-start = (f32[2,2,128,128]{3,2,1,0:T(8,128)}, f32[2,2,128,128]{3,2,1,0:T(8,128)S(1)}, u32[]{:S(2)}) copy-start(f32[2,2,128,128]{3,2,1,0:T(8,128)S(1)} %collective-permute-done.7.refs_0_) | copy-start | bytes 786436
  115.3 4.2 %copy-start.3 = (f32[2,2,128,128]{3,2,1,0:T(8,128)}, f32[2,2,128,128]{3,2,1,0:T(8,128)S(1)}, u32[]{:S(2)}) copy-start(f32[2,2,128,128]{3,2,1,0:T(8,128)S(1)} %collective-permute-done.8.refs_1_) | copy-start | bytes 786436
  119.5 0.7 copy-start.6
